TPU v7x, 128 devices: a whole 4x4x4 slice. The times are simulated.
128 devices in a mesh: dp: 16 (over y, z_hi, core), seq: 8 (over x, z_lo).
Axes of the slice: x: 4, y: 4, z: 4 (z_hi: 2, z_lo: 2; z = z_hi * 2 + z_lo), core: 2. Of those that a mesh axis runs over, the one named last changes fastest.
Arguments:
- tokens: bfloat16 [16, 2048, 1024], P('dp', 'seq'), may hold values from -6 to 6
- proj_weight: bfloat16 [1024, 4096], replicated, may hold values from -0.1875 to 0.1875
- out_weight: bfloat16 [1024, 1024], replicated, may hold values from -0.1875 to 0.1875
- rel_bias: float32 [8, 128], replicated, may hold values from -4 to 4
- segment_ids: int32 [16, 2048], P('dp'), may hold values from 0 to 3, never falling along the last dimension, each value on 1 to 1024 neighbouring positions
- distance_bucket: int32 [2048], replicated, may hold values from 0 to 127
- out_grad: bfloat16 [16, 2048, 1024], P('dp', 'seq'), may hold values from -6 to 6
Outputs:
- layer_out: bfloat16 [16, 2048, 1024], P('dp', 'seq')
- input_grad: bfloat16 [16, 2048, 1024], P('dp', 'seq')
- proj_grad: float32 [1024, 4096], P(('dp', 'seq'))
- out_weight_grad: float32 [1024, 1024], P(('dp', 'seq'))
Inputs may be any that keep to these rules, and one draw needn't show every extreme that they name: `segment_ids`: ids never fall along a row; each history is 1 to 1024 positions long, and one history of every row has exactly 1024 positions.
All inputs are finite; a program needn't handle non-finite values.
Results may differ from a plain program's by a relative error of at most 0.0095.
Values may be sent and summed in bfloat16 or wider, within the bound.
No kernel may reach another device: no remote copies, remote signals or barrier semaphores. Data moves between devices by JAX's collectives and lax.ppermute only.
A program may use at most 704 MiB of HBM per device.

v0:
```python
import functools
import jax
import jax.numpy as jnp
from jax import lax
from jax.experimental import pallas as pl
from jax.experimental.pallas import tpu as pltpu
from jax.sharding import PartitionSpec as P

EPS = 1e-05
TILE = 256
DEAD = -1e30
F32 = jnp.float32
BF16 = jnp.bfloat16


def layer_norm(values):
    average = jnp.mean(values, axis=-1, keepdims=True)
    centered = values - average
    inverse = lax.rsqrt(jnp.mean(centered * centered, axis=-1, keepdims=True) + EPS)
    return centered * inverse, inverse


def dot_nn(left, right):
    return lax.dot_general(left, right, (((1,), (0,)), ((), ())), preferred_element_type=F32)


def dot_nt(left, right):
    return lax.dot_general(left, right, (((1,), (1,)), ((), ())), preferred_element_type=F32)


def dot_tn(left, right):
    return lax.dot_general(left, right, (((0,), (0,)), ((), ())), preferred_element_type=F32)


class Incoming:
    def __init__(self, far, near, sems, first, parts):
        self.near = near
        self.size = near.shape[0] // parts
        self.copies = []
        for part in range(parts):
            rows = pl.ds(part * self.size, self.size)
            self.copies.append(
                pltpu.make_async_copy(far.at[rows], near.at[rows], sems.at[first + part])
            )
        self.pending = [True] * parts

    def start(self, part):
        if part < len(self.copies):
            self.copies[part].start()

    def wait(self, part):
        if part < len(self.copies) and self.pending[part]:
            self.copies[part].wait()
            self.pending[part] = False

    def ready(self):
        for part in range(len(self.copies)):
            self.wait(part)
        return self.near


class Outgoing:
    def __init__(self, near, far, sems, first, parts):
        self.ref = near
        size = near.shape[0] // parts
        self.copies = []
        for part in range(parts):
            rows = pl.ds(part * size, size)
            self.copies.append(
                pltpu.make_async_copy(near.at[rows], far.at[rows], sems.at[first + part])
            )
        self.sent = [False] * parts

    def send(self, part=None):
        if part is not None and len(self.copies) == 1:
            return
        for index, copy in enumerate(self.copies):
            if part in (None, index) and not self.sent[index]:
                copy.start()
                self.sent[index] = True

    def finish(self):
        for copy in self.copies:
            copy.wait()


def call(body, outs, name, smem=0, scratch=(), flops=0, far=(), parts=None, out_parts=None, limit=58, light=False):
    parts = parts or {}
    out_parts = out_parts or {}

    def run(*args):
        size = sum(a.size * a.dtype.itemsize for a in args)
        size += sum(o.size * o.dtype.itemsize for o in outs)
        near_in = [i for i in range(smem, len(args)) if i not in far]
        counts = [parts.get(i, 1) for i in near_in]
        kept = [pltpu.VMEM(args[i].shape, args[i].dtype) for i in near_in]
        kept += [pltpu.VMEM(out.shape, out.dtype) for out in outs]
        out_counts = [out_parts.get(i, 1) for i in range(len(outs))]
        kept += [pltpu.SemaphoreType.DMA((sum(counts),)), pltpu.SemaphoreType.DMA((sum(out_counts),))]

        def kernel(*refs):
            ins, refs = refs[: len(args)], refs[len(args) :]
            far_outs, refs = refs[: len(outs)], refs[len(outs) :]
            near, refs = refs[: len(near_in)], refs[len(near_in) :]
            near_outs, refs = refs[: len(outs)], refs[len(outs) :]
            in_sems, out_sems, extra = refs[0], refs[1], refs[2:]
            values = list(ins)
            first = 0
            for place, ref, count in zip(near_in, near, counts):
                values[place] = Incoming(ins[place], ref, in_sems, first, count)
                first += count
            for part in range(max(counts)):
                for place in near_in:
                    values[place].start(part)
            results = []
            first = 0
            for ref, away, count in zip(near_outs, far_outs, out_counts):
                results.append(Outgoing(ref, away, out_sems, first, count))
                first += count
            body(*values, *results, *extra)
            for place in near_in:
                values[place].ready()
            for result in results:
                result.send()
            for result in results:
                result.finish()

        return pl.pallas_call(
            kernel,
            out_shape=outs,
            in_specs=[pl.BlockSpec(memory_space=pltpu.SMEM)] * smem
            + [pl.BlockSpec(memory_space=pltpu.HBM)] * (len(args) - smem),
            out_specs=[pl.BlockSpec(memory_space=pltpu.HBM)] * len(outs),
            scratch_shapes=kept + list(scratch),
            compiler_params=pltpu.CompilerParams(vmem_limit_bytes=limit * 1024 * 1024),
            cost_estimate=pl.CostEstimate(flops=flops, bytes_accessed=0 if light else size, transcendentals=0),
            name=name,
        )(*args)

    return run


def shape(dims, kind):
    return jax.ShapeDtypeStruct(dims, kind)


def norm_kernel(token, half):
    for part in range(len(token.copies)):
        token.wait(part)
        rows = slice(part * token.size, (part + 1) * token.size)
        normed, _ = layer_norm(token.near[rows, :].astype(F32))
        half.ref[rows, :] = normed.astype(BF16)
        half.send(part)


def prepare_kernel(me_smem, up, half, out_w, weight_far, gg, gate, weight, gate_w, sems):
    width = gate_w.shape[0]
    head = weight.ref.shape[1] // 3
    copies = [pltpu.make_async_copy(weight_far.at[:, :width], gate_w, sems.at[0])]
    for part in range(3):
        start = pl.multiple_of((part + 1) * width + me_smem[0] * head, head)
        source = weight_far.at[:, pl.ds(start, head)]
        target = weight.ref.at[:, part * head : (part + 1) * head]
        copies.append(pltpu.make_async_copy(source, target, sems.at[part + 1]))
    for copy in copies:
        copy.start()
    gg.ref[...] = dot_nt(up.ready()[...], out_w.ready()[...])
    gg.send()
    copies[0].wait()
    gate.ref[...] = dot_nn(half.ready()[...], gate_w[...])
    gate.send()
    for copy in copies[1:]:
        copy.wait()


def bias_tiles(table_ref, tile_ref, turned):
    count = tile_ref.shape[0]
    key_at = lax.broadcasted_iota(jnp.int32, (TILE, TILE), 0)
    query_at = lax.broadcasted_iota(jnp.int32, (TILE, TILE), 1)
    for step in range(count):
        if step < count - 1:
            later = table_ref[:, step * TILE : (step + 1) * TILE]
        else:
            later = jnp.zeros((1, TILE), F32)
        if step > 0:
            earlier = table_ref[:, (step - 1) * TILE : step * TILE]
        else:
            earlier = jnp.zeros((1, TILE), F32)
        window = jnp.broadcast_to(jnp.concatenate([later, earlier], axis=1), (TILE, 2 * TILE))
        rolled = 0.5 * pltpu.roll(window, 0, 1, stride=1, stride_axis=0)[:, :TILE]
        if step == 0:
            rolled = jnp.where(key_at <= query_at, rolled, DEAD)
        tile_ref[step] = rolled if turned else rolled.T


def key_mask(mask):
    return ((1.0 - mask.astype(F32)) * DEAD).astype(BF16)


def forward_kernel(scale, start_smem, *refs):
    weight, table, mask = refs[:3]
    pieces = refs[3 : PIECES + 3]
    feature, slope, attended, bias_ref, key_ref = refs[PIECES + 3 :]
    feature_ref, slope_ref = feature.ref, slope.ref
    count, _, head = attended.ref.shape
    reach = bias_ref.shape[0] - 1
    row_at = lax.broadcasted_iota(jnp.int32, (16, HALF), 0)
    bias_tiles(table.ready(), bias_ref, False)
    mask_ref = mask.ready()
    key_ref[:, head:] = key_mask(mask_ref[...])
    weight_ref = weight.ready()
    for index, piece in enumerate(pieces):
        ref = piece.ready()
        rows = pl.ds(pl.multiple_of(start_smem[index], HALF), ref.shape[0])
        half = 0.5 * dot_nn(ref[...], weight_ref[...])
        lean = jnp.tanh(half)
        rise = 1.0 + lean
        made = (half * rise).astype(BF16)
        feature_ref[rows, :] = made
        key_ref[rows, :head] = made[:, 2 * head :]
        slope_ref[rows, :] = (0.5 * rise * (1.0 + half * (1.0 - lean))).astype(BF16)
    feature.send()
    slope.send()
    for q_block in range(count):
        rows = slice(q_block * TILE, (q_block + 1) * TILE)
        query = jnp.concatenate([feature_ref[rows, head : 2 * head], mask_ref[rows, :]], axis=1)
        total = jnp.zeros((TILE, head), F32)
        for k_block in range(max(0, q_block - reach), q_block + 1):
            k_rows = slice(k_block * TILE, (k_block + 1) * TILE)
            half = dot_nt(query, key_ref[k_rows, :]) * (0.5 * scale) + bias_ref[q_block - k_block]
            weights = half * (1.0 + jnp.tanh(half))
            total = total + dot_nn(weights.astype(BF16), feature_ref[k_rows, :head])
        average = jnp.mean(total, axis=1, keepdims=True)
        attended.ref[q_block, :TILE, :] = (total - average).astype(BF16)
        wide = jnp.broadcast_to(average, total.shape).T[:16, :]
        high = wide.astype(BF16).astype(F32)
        low = wide - high
        packed = jnp.where(row_at == 0, high[:, :HALF], high[:, HALF:])
        packed = jnp.where(row_at == 2, low[:, :HALF], packed)
        packed = jnp.where(row_at == 3, low[:, HALF:], packed)
        attended.ref[q_block, TILE:, :] = packed.astype(BF16)
        attended.send(q_block)


def split_cells(core, total, cell):
    low = [total[2 * k * cell : (2 * k + 1) * cell] for k in range(2)]
    high = [total[(2 * k + 1) * cell : (2 * k + 2) * cell] for k in range(2)]
    mine = [jnp.where(core == 0, x, y) for x, y in zip(low, high)]
    other = [jnp.where(core == 0, y, x) for x, y in zip(low, high)]
    return mine, other


def mix_kernel(
    attended_in, gate_in, gg_in, send_out, gate_grad_out, gated_out
):
    attended_ref = attended_in.ready()
    send_ref = send_out.ref
    heads, _, head = attended_ref.shape
    rows = []
    for index in range(heads):
        packed = attended_ref[index, TILE:, :].astype(F32)
        rows.append(
            jnp.concatenate([packed[0:1] + packed[2:3], packed[1:2] + packed[3:4]], axis=1)
        )
    averages = jnp.concatenate(rows, axis=0).T
    attended = jnp.concatenate(
        [
            attended_ref[index, :TILE, :].astype(F32) + averages[:, index : index + 1]
            for index in range(heads)
        ],
        axis=1,
    )
    mixed, inverse = layer_norm(attended)
    half = 0.5 * gate_in.ready()[...]
    lean = jnp.tanh(half)
    rise = 1.0 + lean
    gate = (half * rise).astype(BF16).astype(F32)
    gg = gg_in.ready()[...]
    gated_out.ref[...] = (mixed * gate).astype(BF16)
    gate_grad = (gg * mixed * (0.5 * rise * (1.0 + half * (1.0 - lean)))).astype(BF16)
    gate_grad_out.ref[...] = gate_grad
    gate_grad_out.send()
    grad = gg * gate
    first = jnp.mean(grad, axis=-1, keepdims=True)
    second = jnp.mean(grad * mixed, axis=-1, keepdims=True)
    grad = ((grad - first - mixed * second) * inverse).astype(BF16)
    for index in range(heads):
        columns = slice(index * head, (index + 1) * head)
        send_ref[index, :, :head] = grad[:, columns]
        send_ref[index, :, head:] = gate_grad[:, columns]


def backward_kernel(
    scale, table, mask, feature, grad_in, slope_in, out, key_sum, value_sum, bias_ref, key_ref
):
    head = key_sum.shape[1]
    out_ref = out.ref
    bias_tiles(table.ready(), bias_ref, True)
    mask_ref, feature_ref = mask.near, feature.near
    grad_ref, slope_ref = grad_in.near, slope_in.near
    count = grad_ref.shape[0]
    reach = bias_ref.shape[0] - 1
    for q_block in range(count):
        rows = slice(q_block * TILE, (q_block + 1) * TILE)
        if q_block % 2 == 0:
            for source in (mask, feature, grad_in):
                source.wait(q_block // 2)
        key_ref[rows, :head] = feature_ref[rows, 2 * head :]
        key_ref[rows, head:] = key_mask(mask_ref[rows, :])
        query_half = feature_ref[rows, head : 2 * head]
        query = jnp.concatenate([query_half, mask_ref[rows, :]], axis=1)
        upstream = grad_ref[q_block, :, :head]
        total = jnp.zeros((TILE, head), F32)
        for k_block in range(max(0, q_block - reach), q_block + 1):
            k_rows = slice(k_block * TILE, (k_block + 1) * TILE)
            key_half = feature_ref[k_rows, 2 * head :]
            half = dot_nt(key_ref[k_rows, :], query) * (0.5 * scale) + bias_ref[q_block - k_block]
            lean = jnp.tanh(half)
            rise = 1.0 + lean
            weight = (half * rise).astype(BF16)
            grad_weight = dot_nt(feature_ref[k_rows, :head], upstream)
            grad_score = (grad_weight * (rise * (1.0 + half * (1.0 - lean)))).astype(BF16)
            value_term = dot_nn(weight, upstream)
            key_term = dot_nn(grad_score, query_half)
            if q_block == k_block:
                value_sum[k_rows, :] = value_term
                key_sum[k_rows, :] = key_term
            else:
                value_sum[k_rows, :] += value_term
                key_sum[k_rows, :] += key_term
            total = total + dot_tn(grad_score, key_half)
        slope_in.wait(q_block)
        slope = slope_ref[rows, head : 2 * head].astype(F32)
        out_ref[q_block, :, head : 2 * head] = (total * (0.5 * scale) * slope).astype(BF16)
        done = [q_block - reach] if q_block < count - 1 else range(q_block - reach, count)
        for block in done:
            if block < 0:
                continue
            rows = slice(block * TILE, (block + 1) * TILE)
            value_slope = slope_ref[rows, :head].astype(F32)
            key_slope = slope_ref[rows, 2 * head :].astype(F32)
            out_ref[block, :, :head] = (value_sum[rows, :] * value_slope).astype(BF16)
            key_grad = key_sum[rows, :] * (0.5 * scale) * key_slope
            out_ref[block, :, 2 * head :] = key_grad.astype(BF16)
            if block == count // 2 - 1:
                out.send(0)


def sums_kernel(info_smem, *refs):
    mix, grad = refs[:2]
    pieces = refs[2 : PIECES + 2]
    gated, up, out_w, token, mine_out = refs[PIECES + 2 : PIECES + 7]
    others, layer, right_ref = refs[PIECES + 7 : -2], refs[-2], refs[-1]
    core = info_smem[PIECES]
    cell = TILE // 4
    mix_ref, grad_ref = mix.ready(), grad.ready()
    head = grad_ref.shape[2] // 3
    for block in range(grad_ref.shape[0]):
        rows = slice(block * TILE, (block + 1) * TILE)
        right_ref[rows, :head] = mix_ref[block, :, head:]
        right_ref[rows, head:] = grad_ref[block]
    for chunk in range(pieces[0].near.shape[1] // TILE):
        columns = slice(chunk * TILE, (chunk + 1) * TILE)
        total = jnp.zeros((TILE, 4 * head), F32)
        for index, piece in enumerate(pieces):
            ref = piece.ready()
            rows = pl.ds(pl.multiple_of(info_smem[index], HALF), ref.shape[0])
            total = total + dot_tn(ref[:, columns], right_ref[rows, :])
        mine, other = split_cells(core, total, cell)
        for index in range(2):
            mine_out.ref[2 * chunk + index, :, : 4 * head] = mine[index].astype(BF16)
            others[0].ref[2 * chunk + index] = other[index].astype(BF16)
    others[0].send()
    gated_ref = gated.ready()
    up_rows = up.ready()[...]
    for chunk in range(gated_ref.shape[1] // TILE):
        total = dot_tn(gated_ref[:, chunk * TILE : (chunk + 1) * TILE], up_rows)
        mine, other = split_cells(core, total, cell)
        for index in range(2):
            mine_out.ref[2 * chunk + index, :, 4 * head :] = mine[index].astype(BF16)
            for out, first in zip(others[1:], (0, 4 * head)):
                columns = slice(first, first + 4 * head)
                out.ref[2 * chunk + index] = other[index][:, columns].astype(BF16)
    mine_out.send()
    for out in others[1:]:
        out.send()
    result = dot_nn(gated_ref[...], out_w.ready()[...])
    layer.ref[...] = (token.ready()[...].astype(F32) + result).astype(BF16)


def join_kernel(mine, *refs):
    others, out = refs[:-1], refs[-1]
    mine_ref = mine.ready()
    first = 0
    for other in others:
        ref = other.ready()
        columns = slice(first, first + ref.shape[2])
        total = mine_ref[:, :, columns].astype(F32) + ref[...].astype(F32)
        out.ref[:, :, columns] = total.astype(BF16)
        first += ref.shape[2]


def input_kernel(gate_grad, grad_in, weight, token, up, out, all_grad, total):
    grad_ref = grad_in.ready()
    heads = grad_ref.shape[0]
    head = grad_ref.shape[2] // 3
    width = heads * head
    all_grad[:, :width] = gate_grad.ready()[...]
    for index in range(heads):
        for part in range(3):
            start = (part + 1) * width + index * head
            all_grad[:, start : start + head] = grad_ref[index, :, part * head : (part + 1) * head]
    for step in range(width // TILE):
        part = slice(step * TILE, (step + 1) * TILE)
        weight.wait(step)
        total[:, part] = dot_nt(all_grad[...], weight.near[part, :])
    grad = total[...]
    normed, inverse = layer_norm(token.ready()[...].astype(F32))
    first = jnp.mean(grad, axis=-1, keepdims=True)
    second = jnp.mean(grad * normed, axis=-1, keepdims=True)
    back = (grad - first - normed * second) * inverse
    out.ref[...] = (up.ready()[...].astype(F32) + back).astype(BF16)


def shift(values, by):
    return lax.ppermute(values, "seq", [(index, (index + by) % 8) for index in range(8)])


def swap(values, axis, bits, size):
    return lax.ppermute(values, axis, [(index, index ^ bits) for index in range(size)])


def gather_first(own):
    return swap(own, "seq", 1, 8), shift(own, -2), shift(own, 2)


def gather_rest(own, mate, after, before):
    half = own.shape[0] // 2
    across_low = shift(after[:half], -2)
    across_high = shift(before[half:], 2)
    mate_before = swap(before, "seq", 1, 8)
    mate_after = shift(mate, -2)
    mate_across_low = swap(across_low, "seq", 1, 8)
    mate_across_high = shift(mate_before[half:], 2)
    me = lax.axis_index("seq").astype(jnp.int32)
    other = me ^ 1
    pieces = [
        (own, me, 0),
        (mate, other, 0),
        (after, me + 2, 0),
        (before, me + 6, 0),
        (across_low, me + 4, 0),
        (across_high, me + 4, half),
        (mate_before, other + 6, 0),
        (mate_after, other + 2, 0),
        (mate_across_low, other + 4, 0),
        (mate_across_high, other + 4, half),
    ]
    starts = [(place % 8) * own.shape[0] + first for _, place, first in pieces]
    return [piece for piece, _, _ in pieces], starts


PIECES = 10
HALF = TILE // 2


CHIPS = [
    [place * 8 + part for place in range(core, 16, 2) for part in range(8)] for core in range(2)
]


def exchange_chips(values):
    return lax.all_to_all(values, ("dp", "seq"), 0, 0, axis_index_groups=CHIPS)


def exchange(values):
    return lax.all_to_all(values, "seq", 0, 0)


def per_device(tokens, proj_weight, out_weight, rel_bias, segment_ids, distance_bucket, out_grad):
    heads, buckets = rel_bias.shape
    rows, width = tokens.shape[1:]
    head = width // heads
    length = segment_ids.shape[1]
    scale = head ** (-0.5)
    reach = 1024 // TILE
    me = lax.axis_index("seq").astype(jnp.int32)
    core = (lax.axis_index("dp") % 2).astype(jnp.int32)
    token_row = tokens[0]
    upstream = out_grad[0]

    half = call(
        norm_kernel, [shape((rows, width), BF16)], "norm"
    )(token_row)[0]
    near = gather_first(half)

    gg, gate_proj, weight = call(
        prepare_kernel,
        [shape((rows, width), F32), shape((rows, width), F32), shape((width, 3 * head), BF16)],
        "prepare",
        smem=1,
        far=(4,),
        scratch=[pltpu.VMEM((width, width), BF16), pltpu.SemaphoreType.DMA((4,))],
        flops=4 * rows * width * width,
    )(me[None], upstream, half, out_weight, proj_weight)
    one_hot = (
        distance_bucket[None, : reach * TILE] == jnp.arange(buckets, dtype=jnp.int32)[:, None]
    ).astype(F32)
    table = jnp.dot(
        lax.dynamic_slice_in_dim(rel_bias, me, 1, 0),
        one_hot,
        precision=lax.Precision.HIGHEST,
        preferred_element_type=F32,
    )
    mask = (segment_ids[0][:, None] == jnp.arange(128, dtype=jnp.int32)[None, :]).astype(BF16)
    near, gg, gate_proj, weight, table, mask = lax.optimization_barrier(
        (near, gg, gate_proj, weight, table, mask)
    )
    pieces, starts = gather_rest(half, *near)
    info = lax.optimization_barrier(jnp.stack(starts + [core]))

    tiles = pltpu.VMEM((reach + 1, TILE, TILE), F32)
    features, slopes, attended = call(
        functools.partial(forward_kernel, scale),
        [
            shape((length, 3 * head), BF16),
            shape((length, 3 * head), BF16),
            shape((8, rows + 16, head), BF16),
        ],
        "forward",
        smem=1,
        out_parts={2: 8},
        scratch=[tiles, pltpu.VMEM((length, 2 * head), BF16)],
        flops=2 * length * width * 4 * head,
    )(info, weight, table, mask, *pieces)
    attended_own = exchange(attended)

    row_shape = shape((rows, width), BF16)
    send, gate_grad, gated = call(
        mix_kernel,
        [shape((heads, rows, 2 * head), BF16), row_shape, row_shape],
        "mix",
    )(attended_own, gate_proj, gg)
    mix_head = exchange(send)

    grads = call(
        functools.partial(backward_kernel, scale),
        [shape((8, rows, 3 * head), BF16)],
        "backward",
        parts={1: 4, 2: 4, 3: 4},
        out_parts={0: 2},
        scratch=[
            pltpu.VMEM((length, head), F32),
            pltpu.VMEM((length, head), F32),
            tiles,
            pltpu.VMEM((length, 2 * head), BF16),
        ],
        flops=10 * length * 4096 * head,
    )(table, mask, features, mix_head, slopes)[0]
    grads_own = exchange(grads)

    cells = shape((8, width // 16, 4 * head + width), BF16)
    third = shape((8, width // 16, 4 * head), BF16)
    mine, first, second, last, layer_row = call(
        sums_kernel,
        [cells, third, third, third, row_shape],
        "sums",
        smem=1,
        scratch=[pltpu.VMEM((length, 4 * head), BF16)],
        flops=2 * length * width * 4 * head + 4 * rows * width * width,
    )(info, mix_head, grads, *pieces, gated, upstream, out_weight, token_row)
    others = [swap(part, "dp", 1, 16) for part in (first, second, last)]
    both = call(join_kernel, [cells], "join", light=True)(mine, *others)[0]
    both, grads_own = lax.optimization_barrier((both, grads_own))
    few = width // 128
    parts = exchange_chips(both.reshape(64, few, 4 * head + width))
    final = jnp.sum(parts.reshape(8, 8, few, -1).astype(F32), axis=0)
    proj_out = final[:, :, : 4 * head].reshape(8, few, 4, head)
    proj_out = proj_out.transpose(1, 2, 0, 3).reshape(few, 4 * width)
    out_out = jnp.sum(final[:, :, 4 * head :], axis=0)

    grad_row = call(
        input_kernel,
        [shape((rows, width), BF16)],
        "input_grad",
        parts={2: width // TILE},
        scratch=[pltpu.VMEM((rows, 4 * width), BF16), pltpu.VMEM((rows, width), F32)],
        flops=8 * rows * width * width,
    )(gate_grad, grads_own, proj_weight, token_row, upstream)[0]
    return layer_row[None], grad_row[None], proj_out, out_out


def solution(mesh):
    return jax.shard_map(
        per_device,
        mesh=mesh,
        in_specs=(P("dp", "seq", None), P(), P(), P(), P("dp", None), P(), P("dp", "seq", None)),
        out_specs=(
            P("dp", "seq", None),
            P("dp", "seq", None),
            P(("dp", "seq"), None),
            P(("dp", "seq"), None),
        ),
        check_vma=False,
    )
```

profile of v0, /device:TPU:0, one launch (start us, length us, event | category | flops | bytes accessed | tf_op | source)
XLA Modules:
  0.0 158.9 jit_solution(16953688863136533463)
XLA Ops:
  0.6 2.2 %norm.1.refs_2_.refs_4_.refs_3_ = bf16[256,1024]{1,0:T(8,128)(2,1)} custom-call(bf16[256,1024]{1,0:T(8,128)(2,1)} %bitcast.41), custom_call_target="tpu_custom_call" | custom-call | bytes 1048576 | tf_op jit(solution)/shard_map/norm/pallas_call | solution.py:128
  2.8 1.6 %collective-permute-start.2 = (bf16[256,1024]{1,0:T(8,128)(2,1)}, bf16[256,1024]{1,0:T(8,128)(2,1)S(1)}, u32[]{:S(2)}, u32[]{:S(2)}) collective-permute-start(bf16[256,1024]{1,0:T(8,128)(2,1)} %norm.1.refs_2_.refs_4_.refs_3_), channel_id=1, source_target_pairs={{0,2},{1,3},{2,4},{3,5},{4,6},{5,7},{6,0},{7,1},{8,10},{9,11},{10,... | collective-permute-start | bytes 1572872 | tf_op jit(solution)/shard_map/ppermute | solution.py:426
  4.5 1.7 %collective-permute-start.1 = (bf16[256,1024]{1,0:T(8,128)(2,1)}, bf16[256,1024]{1,0:T(8,128)(2,1)S(1)}, u32[]{:S(2)}, u32[]{:S(2)}) collective-permute-start(bf16[256,1024]{1,0:T(8,128)(2,1)} %norm.1.refs_2_.refs_4_.refs_3_), channel_id=1, source_target_pairs={{0,6},{1,7},{2,0},{3,1},{4,2},{5,3},{6,4},{7,5},{8,14},{9,15},{10,... | collective-permute-start | bytes 1572872 | tf_op jit(solution)/shard_map/ppermute | solution.py:426
  6.1 2.0 %collective-permute-start = (bf16[256,1024]{1,0:T(8,128)(2,1)}, bf16[256,1024]{1,0:T(8,128)(2,1)S(1)}, u32[]{:S(2)}, u32[]{:S(2)}) collective-permute-start(bf16[256,1024]{1,0:T(8,128)(2,1)} %norm.1.refs_2_.refs_4_.refs_3_), channel_id=1, source_target_pairs={{0,1},{1,0},{2,3},{3,2},{4,5},{5,4},{6,7},{7,6},{8,9},{9,8},{10,11... | collective-permute-start | bytes 1572872 | tf_op jit(solution)/shard_map/ppermute | solution.py:430
  9.7 5.6 %prepare.1 = (f32[256,1024]{1,0:T(8,128)}, f32[256,1024]{1,0:T(8,128)}, bf16[1024,384]{1,0:T(8,128)(2,1)}) custom-call(s32[1]{0:T(128)} %bitcast.12.refs_0_, bf16[256,1024]{1,0:T(8,128)(2,1)} %bitcast.38, bf16[256,1024]{1,0:T(8,128)(2,1)} %norm.1.refs_2_.refs_4_.refs_3_, bf16[1024,1024]{1,0:T(8,128)(2,1)} %refs_15_.1, bf16[1024,4096]{1,0:T(8,128)(2,1)} %refs_2_.1), custom_call_target="tpu_custom_call" | custom-call | flops 1073741824 | bytes 14417924 | tf_op jit(solution)/shard_map/prepare/pallas_call | solution.py:128
  18.1 1.7 %collective-permute-done.refs_5_.refs_4_ = bf16[256,1024]{1,0:T(8,128)(2,1)S(1)} collective-permute-done((bf16[256,1024]{1,0:T(8,128)(2,1)}, bf16[256,1024]{1,0:T(8,128)(2,1)S(1)}, u32[]{:S(2)}, u32[]{:S(2)}) %collective-permute-start) | collective-permute-done | bytes 524320 | tf_op jit(solution)/shard_map/ppermute | solution.py:430
  19.7 1.7 %collective-permute-start.5 = (bf16[256,1024]{1,0:T(8,128)(2,1)S(1)}, bf16[256,1024]{1,0:T(8,128)(2,1)S(1)}, u32[]{:S(2)}, u32[]{:S(2)}) collective-permute-start(bf16[256,1024]{1,0:T(8,128)(2,1)S(1)} %collective-permute-done.2.refs_7_.refs_6_), channel_id=1, source_target_pairs={{0,1},{1,0},{2,3},{3,2},{4,5},{5,4},{6,7},{7,6},{8,9},{9,8},{10,11... | collective-permute-start | bytes 1572872 | tf_op jit(solution)/shard_map/ppermute | solution.py:430
  21.5 1.6 %collective-permute-start.3 = (bf16[128,1024]{1,0:T(8,128)(2,1)S(1)}, bf16[128,1024]{1,0:T(8,128)(2,1)S(1)}, u32[]{:S(2)}, u32[]{:S(2)}) collective-permute-start(bf16[128,1024]{1,0:T(8,128)(2,1)S(1)} %slice.19), channel_id=1, source_target_pairs={{0,6},{1,7},{2,0},{3,1},{4,2},{5,3},{6,4},{7,5},{8,14},{9,15},{10,... | collective-permute-start | bytes 786440 | tf_op jit(solution)/shard_map/ppermute | solution.py:426
  25.2 5.6 %collective-permute-done.3.refs_8_.refs_7_ = bf16[128,1024]{1,0:T(8,128)(2,1)S(1)} collective-permute-done((bf16[128,1024]{1,0:T(8,128)(2,1)S(1)}, bf16[128,1024]{1,0:T(8,128)(2,1)S(1)}, u32[]{:S(2)}, u32[]{:S(2)}) %collective-permute-start.3) | collective-permute-done | bytes 262176 | tf_op jit(solution)/shard_map/ppermute | solution.py:426
  31.1 3.5 %collective-permute-done.5.refs_10_.refs_9_ = bf16[256,1024]{1,0:T(8,128)(2,1)S(1)} collective-permute-done((bf16[256,1024]{1,0:T(8,128)(2,1)S(1)}, bf16[256,1024]{1,0:T(8,128)(2,1)S(1)}, u32[]{:S(2)}, u32[]{:S(2)}) %collective-permute-start.5) | collective-permute-done | bytes 524320 | tf_op jit(solution)/shard_map/ppermute | solution.py:430
  35.8 2.1 %collective-permute-done.7.refs_12_.refs_11_ = bf16[128,1024]{1,0:T(8,128)(2,1)} collective-permute-done((bf16[128,1024]{1,0:T(8,128)(2,1)S(1)}, bf16[128,1024]{1,0:T(8,128)(2,1)}, u32[]{:S(2)}, u32[]{:S(2)}) %collective-permute-start.7) | collective-permute-done | bytes 262176 | tf_op jit(solution)/shard_map/ppermute | solution.py:430
  39.0 3.5 %collective-permute-done.8.refs_13_.refs_12_ = bf16[128,1024]{1,0:T(8,128)(2,1)} collective-permute-done((bf16[128,1024]{1,0:T(8,128)(2,1)S(1)}, bf16[128,1024]{1,0:T(8,128)(2,1)}, u32[]{:S(2)}, u32[]{:S(2)}) %collective-permute-start.8) | collective-permute-done | bytes 262176 | tf_op jit(solution)/shard_map/ppermute | solution.py:426
  42.6 11.5 %forward.1 = (bf16[2048,384]{1,0:T(8,128)(2,1)}, bf16[2048,384]{1,0:T(8,128)(2,1)}, bf16[8,272,128]{2,1,0:T(8,128)(2,1)}) custom-call(s32[11]{0:T(128)} %stack.47.refs_0_, bf16[1024,384]{1,0:T(8,128)(2,1)} %get-tuple-element.31.refs_1_, f32[1,1024]{1,0:T(1,128)} %fusion.1.refs_2_.refs_0_, bf16[2048,128]{1,0:T(8,128)(2,1)} %fusion.refs_3_.refs_1_, ...), custom_call_target="tpu_custom_call" | custom-call | flops 2147483648 | bytes 9211948 | tf_op jit(solution)/shard_map/forward/pallas_call | solution.py:128
  54.1 13.2 %all_to_all.20.refs_0_ = bf16[8,272,128]{2,1,0:T(8,128)(2,1)} all-to-all(bf16[8,272,128]{2,1,0:T(8,128)(2,1)} %get-tuple-element.37), channel_id=1, replica_groups=mesh['dp'=16,'seq'=8] {'seq'}, dimensions={0} | all-to-all | bytes 1114112 | tf_op jit(solution)/shard_map/all_to_all | solution.py:477
  67.3 4.3 %mix.1 = (bf16[8,256,256]{2,1,0:T(8,128)(2,1)}, bf16[256,1024]{1,0:T(8,128)(2,1)}, bf16[256,1024]{1,0:T(8,128)(2,1)}) custom-call(bf16[8,272,128]{2,1,0:T(8,128)(2,1)} %all_to_all.20.refs_0_, f32[256,1024]{1,0:T(8,128)} %get-tuple-element.38.refs_1_, f32[256,1024]{1,0:T(8,128)} %get-tuple-element.39.refs_2_), custom_call_target="tpu_custom_call" | custom-call | bytes 4751360 | tf_op jit(solution)/shard_map/mix/pallas_call | solution.py:128
  71.6 15.4 %all_to_all.21.refs_3_.refs_1_ = bf16[8,256,256]{2,1,0:T(8,128)(2,1)} all-to-all(bf16[8,256,256]{2,1,0:T(8,128)(2,1)} %get-tuple-element.40), channel_id=1, replica_groups=mesh['dp'=16,'seq'=8] {'seq'}, dimensions={0} | all-to-all | bytes 2097152 | tf_op jit(solution)/shard_map/all_to_all | solution.py:477
  87.0 12.5 %backward.1.refs_2_ = bf16[8,256,384]{2,1,0:T(8,128)(2,1)} custom-call(f32[1,1024]{1,0:T(1,128)} %fusion.1.refs_2_.refs_0_, bf16[2048,128]{1,0:T(8,128)(2,1)} %fusion.refs_3_.refs_1_, bf16[2048,384]{1,0:T(8,128)(2,1)} %get-tuple-element.41.refs_2_, bf16[8,256,256]{2,1,0:T(8,128)(2,1)} %all_to_all.21.refs_3_.refs_1_, bf16[2048,384]{1,0:T(8,128)(2,1)} %get-tuple-element.42.refs_4_), custom_call_target="tpu_custom_call" | custom-call | flops 10737418240 | bytes 6295552 | tf_op jit(solution)/shard_map/backward/pallas_call | solution.py:128
  99.4 3.9 %all-to-all-start.2 = ((bf16[8,256,384]{2,1,0:T(8,128)(2,1)}), bf16[8,256,384]{2,1,0:T(8,128)(2,1)S(1)}, u32[]{:S(2)}, u32[]{:S(2)}) async-start(bf16[8,256,384]{2,1,0:T(8,128)(2,1)} %backward.1.refs_2_), calls=%async_computation.2 | async-start | bytes 3145728 | tf_op jit(solution)/shard_map/all_to_all | solution.py:477
  103.3 8.9 %sums.1 = (bf16[8,64,1536]{2,1,0:T(8,128)(2,1)}, bf16[8,64,512]{2,1,0:T(8,128)(2,1)}, bf16[8,64,512]{2,1,0:T(8,128)(2,1)}, bf16[8,64,512]{2,1,0:T(8,128)(2,1)}, bf16[256,1024]{1,0:T(8,128)(2,1)}) custom-call(s32[11]{0:T(128)} %stack.47.refs_0_, bf16[8,256,256]{2,1,0:T(8,128)(2,1)} %all_to_all.21.refs_3_.refs_1_, bf16[8,256,384]{2,1,0:T(8,128)(2,1)} %backward.1.refs_2_, ...), custom_call_target="tpu_custom_call" | custom-call | flops 3221225472 | bytes 14155820 | tf_op jit(solution)/shard_map/sums/pallas_call | solution.py:128
  112.9 1.5 collective-permute-done.9.refs_1_
  116.7 3.2 %join.1 = bf16[8,64,1536]{2,1,0:T(8,128)(2,1)} custom-call(bf16[8,64,1536]{2,1,0:T(8,128)(2,1)} %get-tuple-element.46.refs_0_, bf16[8,64,512]{2,1,0:T(8,128)(2,1)} %copy-done.2, bf16[8,64,512]{2,1,0:T(8,128)(2,1)} %copy-done.3, bf16[8,64,512]{2,1,0:T(8,128)(2,1)} %copy-done.4), custom_call_target="tpu_custom_call" | custom-call | tf_op jit(solution)/shard_map/join/pallas_call | solution.py:128
  121.1 11.2 %all-to-all-start.3 = ((bf16[64,8,1536]{2,1,0:T(8,128)(2,1)}), bf16[64,8,1536]{2,1,0:T(8,128)(2,1)S(1)}, u32[]{:S(2)}, u32[]{:S(2)}) async-start(bf16[64,8,1536]{2,1,0:T(8,128)(2,1)} %bitcast.36), calls=%async_computation.3 | async-start | bytes 3145728 | tf_op jit(solution)/shard_map/all_to_all | solution.py:473
  132.3 8.8 %input_grad.1 = bf16[256,1024]{1,0:T(8,128)(2,1)} custom-call(bf16[256,1024]{1,0:T(8,128)(2,1)} %get-tuple-element.45.refs_0_, bf16[8,256,384]{2,1,0:T(8,128)(2,1)} %copy-done.1, bf16[1024,4096]{1,0:T(8,128)(2,1)} %refs_2_.1, bf16[256,1024]{1,0:T(8,128)(2,1)} %bitcast.43, bf16[256,1024]{1,0:T(8,128)(2,1)} %bitcast.40), custom_call_target="tpu_custom_call" | custom-call | flops 2147483648 | bytes 12058624 | tf_op jit(solution)/shard_map/input_grad/pallas_call | solution.py:128
  141.1 16.1 %all-to-all-done.3 = bf16[64,8,1536]{2,1,0:T(8,128)(2,1)S(1)} async-done(((bf16[64,8,1536]{2,1,0:T(8,128)(2,1)}), bf16[64,8,1536]{2,1,0:T(8,128)(2,1)S(1)}, u32[]{:S(2)}, u32[]{:S(2)}) %all-to-all-start.3) | async-done | bytes 1572896 | tf_op jit(solution)/shard_map/all_to_all | solution.py:473
  (50 shorter events, 15.0 us)
Async XLA Ops:
  0.6 8.2 %copy-start = (f32[8,128]{1,0:T(8,128)S(1)}, f32[8,128]{1,0:T(8,128)}, u32[]{:S(2)}) copy-start(f32[8,128]{1,0:T(8,128)} %param.10) | copy-start | bytes 12292
  2.8 15.0 %collective-permute-start.2 = (bf16[256,1024]{1,0:T(8,128)(2,1)}, bf16[256,1024]{1,0:T(8,128)(2,1)S(1)}, u32[]{:S(2)}, u32[]{:S(2)}) collective-permute-start(bf16[256,1024]{1,0:T(8,128)(2,1)} %norm.1.refs_2_.refs_4_.refs_3_), channel_id=1, source_target_pairs={{0,2},{1,3},{2,4},{3,5},{4,6},{5,7},{6,0},{7,1},{8,10},{9,11},{10,... | collective-permute-start | bytes 1572872 | tf_op jit(solution)/shard_map/ppermute | solution.py:426
  4.5 13.6 %collective-permute-start.1 = (bf16[256,1024]{1,0:T(8,128)(2,1)}, bf16[256,1024]{1,0:T(8,128)(2,1)S(1)}, u32[]{:S(2)}, u32[]{:S(2)}) collective-permute-start(bf16[256,1024]{1,0:T(8,128)(2,1)} %norm.1.refs_2_.refs_4_.refs_3_), channel_id=1, source_target_pairs={{0,6},{1,7},{2,0},{3,1},{4,2},{5,3},{6,4},{7,5},{8,14},{9,15},{10,... | collective-permute-start | bytes 1572872 | tf_op jit(solution)/shard_map/ppermute | solution.py:426
  6.1 13.6 %collective-permute-start = (bf16[256,1024]{1,0:T(8,128)(2,1)}, bf16[256,1024]{1,0:T(8,128)(2,1)S(1)}, u32[]{:S(2)}, u32[]{:S(2)}) collective-permute-start(bf16[256,1024]{1,0:T(8,128)(2,1)} %norm.1.refs_2_.refs_4_.refs_3_), channel_id=1, source_target_pairs={{0,1},{1,0},{2,3},{3,2},{4,5},{5,4},{6,7},{7,6},{8,9},{9,8},{10,11... | collective-permute-start | bytes 1572872 | tf_op jit(solution)/shard_map/ppermute | solution.py:430
  9.7 5.6 %copy-start.8 = (s32[1,2048]{1,0:T(1,128)S(1)}, s32[1,2048]{1,0:T(1,128)}, u32[]{:S(2)}) copy-start(s32[1,2048]{1,0:T(1,128)} %param.11) | copy-start | bytes 24580
  17.9 24.7 %copy-start.5 = (bf16[256,1024]{1,0:T(8,128)(2,1)}, bf16[256,1024]{1,0:T(8,128)(2,1)S(1)}, u32[]{:S(2)}) copy-start(bf16[256,1024]{1,0:T(8,128)(2,1)S(1)} %collective-permute-done.2.refs_7_.refs_6_) | copy-start | bytes 1572868
  18.1 24.5 %copy-start.6 = (bf16[256,1024]{1,0:T(8,128)(2,1)}, bf16[256,1024]{1,0:T(8,128)(2,1)S(1)}, u32[]{:S(2)}) copy-start(bf16[256,1024]{1,0:T(8,128)(2,1)S(1)} %collective-permute-done.1.refs_6_.refs_5_) | copy-start | bytes 1572868
  19.7 22.8 %copy-start.9 = (bf16[256,1024]{1,0:T(8,128)(2,1)}, bf16[256,1024]{1,0:T(8,128)(2,1)S(1)}, u32[]{:S(2)}) copy-start(bf16[256,1024]{1,0:T(8,128)(2,1)S(1)} %collective-permute-done.refs_5_.refs_4_) | copy-start | bytes 1572868
  19.7 14.9 %collective-permute-start.5 = (bf16[256,1024]{1,0:T(8,128)(2,1)S(1)}, bf16[256,1024]{1,0:T(8,128)(2,1)S(1)}, u32[]{:S(2)}, u32[]{:S(2)}) collective-permute-start(bf16[256,1024]{1,0:T(8,128)(2,1)S(1)} %collective-permute-done.2.refs_7_.refs_6_), channel_id=1, source_target_pairs={{0,1},{1,0},{2,3},{3,2},{4,5},{5,4},{6,7},{7,6},{8,9},{9,8},{10,11... | collective-permute-start | bytes 1572872 | tf_op jit(solution)/shard_map/ppermute | solution.py:430
  21.5 9.3 %collective-permute-start.3 = (bf16[128,1024]{1,0:T(8,128)(2,1)S(1)}, bf16[128,1024]{1,0:T(8,128)(2,1)S(1)}, u32[]{:S(2)}, u32[]{:S(2)}) collective-permute-start(bf16[128,1024]{1,0:T(8,128)(2,1)S(1)} %slice.19), channel_id=1, source_target_pairs={{0,6},{1,7},{2,0},{3,1},{4,2},{5,3},{6,4},{7,5},{8,14},{9,15},{10,... | collective-permute-start | bytes 786440 | tf_op jit(solution)/shard_map/ppermute | solution.py:426
  23.1 15.9 %collective-permute-start.6 = (bf16[256,1024]{1,0:T(8,128)(2,1)S(1)}, bf16[256,1024]{1,0:T(8,128)(2,1)S(1)}, u32[]{:S(2)}, u32[]{:S(2)}) collective-permute-start(bf16[256,1024]{1,0:T(8,128)(2,1)S(1)} %collective-permute-done.refs_5_.refs_4_), channel_id=1, source_target_pairs={{0,6},{1,7},{2,0},{3,1},{4,2},{5,3},{6,4},{7,5},{8,14},{9,15},{10,... | collective-permute-start | bytes 1572872 | tf_op jit(solution)/shard_map/ppermute | solution.py:426
  23.9 11.9 %collective-permute-start.4 = (bf16[128,1024]{1,0:T(8,128)(2,1)S(1)}, bf16[128,1024]{1,0:T(8,128)(2,1)}, u32[]{:S(2)}, u32[]{:S(2)}) collective-permute-start(bf16[128,1024]{1,0:T(8,128)(2,1)S(1)} %slice.20), channel_id=1, source_target_pairs={{0,2},{1,3},{2,4},{3,5},{4,6},{5,7},{6,0},{7,1},{8,10},{9,11},{10,... | collective-permute-start | bytes 786440 | tf_op jit(solution)/shard_map/ppermute | solution.py:426
  30.8 11.8 %copy-start.11 = (bf16[128,1024]{1,0:T(8,128)(2,1)}, bf16[128,1024]{1,0:T(8,128)(2,1)S(1)}, u32[]{:S(2)}) copy-start(bf16[128,1024]{1,0:T(8,128)(2,1)S(1)} %collective-permute-done.3.refs_8_.refs_7_) | copy-start | bytes 786436
  30.8 7.2 %collective-permute-start.7 = (bf16[128,1024]{1,0:T(8,128)(2,1)S(1)}, bf16[128,1024]{1,0:T(8,128)(2,1)}, u32[]{:S(2)}, u32[]{:S(2)}) collective-permute-start(bf16[128,1024]{1,0:T(8,128)(2,1)S(1)} %collective-permute-done.3.refs_8_.refs_7_), channel_id=1, source_target_pairs={{0,1},{1,0},{2,3},{3,2},{4,5},{5,4},{6,7},{7,6},{8,9},{9,8},{10,11... | collective-permute-start | bytes 786440 | tf_op jit(solution)/shard_map/ppermute | solution.py:430
  34.6 8.0 %copy-start.7 = (bf16[256,1024]{1,0:T(8,128)(2,1)}, bf16[256,1024]{1,0:T(8,128)(2,1)S(1)}, u32[]{:S(2)}) copy-start(bf16[256,1024]{1,0:T(8,128)(2,1)S(1)} %collective-permute-done.5.refs_10_.refs_9_) | copy-start | bytes 1572868
  34.6 7.9 %collective-permute-start.8 = (bf16[128,1024]{1,0:T(8,128)(2,1)S(1)}, bf16[128,1024]{1,0:T(8,128)(2,1)}, u32[]{:S(2)}, u32[]{:S(2)}) collective-permute-start(bf16[128,1024]{1,0:T(8,128)(2,1)S(1)} %slice.24), channel_id=1, source_target_pairs={{0,2},{1,3},{2,4},{3,5},{4,6},{5,7},{6,0},{7,1},{8,10},{9,11},{10,... | collective-permute-start | bytes 786440 | tf_op jit(solution)/shard_map/ppermute | solution.py:426
  39.0 3.5 %copy-start.10 = (bf16[256,1024]{1,0:T(8,128)(2,1)}, bf16[256,1024]{1,0:T(8,128)(2,1)S(1)}, u32[]{:S(2)}) copy-start(bf16[256,1024]{1,0:T(8,128)(2,1)S(1)} %collective-permute-done.6.refs_11_.refs_10_) | copy-start | bytes 1572868
  99.4 20.4 %all-to-all-start.2 = ((bf16[8,256,384]{2,1,0:T(8,128)(2,1)}), bf16[8,256,384]{2,1,0:T(8,128)(2,1)S(1)}, u32[]{:S(2)}, u32[]{:S(2)}) async-start(bf16[8,256,384]{2,1,0:T(8,128)(2,1)} %backward.1.refs_2_), calls=%async_computation.2 | async-start | bytes 3145728 | tf_op jit(solution)/shard_map/all_to_all | solution.py:477
  112.2 2.2 %collective-permute-start.9 = (bf16[8,64,512]{2,1,0:T(8,128)(2,1)}, bf16[8,64,512]{2,1,0:T(8,128)(2,1)S(1)}, u32[]{:S(2)}, u32[]{:S(2)}) collective-permute-start(bf16[8,64,512]{2,1,0:T(8,128)(2,1)} %get-tuple-element.47), channel_id=1, source_target_pairs={{0,8},{8,0},{16,24},{24,16},{32,40},{40,32},{48,56},{56,48},{64,72... | collective-permute-start | bytes 1572872 | tf_op jit(solution)/shard_map/ppermute | solution.py:430
  112.3 2.9 %collective-permute-start.10 = (bf16[8,64,512]{2,1,0:T(8,128)(2,1)}, bf16[8,64,512]{2,1,0:T(8,128)(2,1)S(1)}, u32[]{:S(2)}, u32[]{:S(2)}) collective-permute-start(bf16[8,64,512]{2,1,0:T(8,128)(2,1)} %get-tuple-element.48), channel_id=1, source_target_pairs={{0,8},{8,0},{16,24},{24,16},{32,40},{40,32},{48,56},{56,48},{64,72... | collective-permute-start | bytes 1572872 | tf_op jit(solution)/shard_map/ppermute | solution.py:430
  112.8 3.1 %collective-permute-start.11 = (bf16[8,64,512]{2,1,0:T(8,128)(2,1)}, bf16[8,64,512]{2,1,0:T(8,128)(2,1)S(1)}, u32[]{:S(2)}, u32[]{:S(2)}) collective-permute-start(bf16[8,64,512]{2,1,0:T(8,128)(2,1)} %get-tuple-element.49), channel_id=1, source_target_pairs={{0,8},{8,0},{16,24},{24,16},{32,40},{40,32},{48,56},{56,48},{64,72... | collective-permute-start | bytes 1572872 | tf_op jit(solution)/shard_map/ppermute | solution.py:430
  114.4 1.5 copy-start.2
  119.9 1.2 copy-start.1
  121.1 36.1 %all-to-all-start.3 = ((bf16[64,8,1536]{2,1,0:T(8,128)(2,1)}), bf16[64,8,1536]{2,1,0:T(8,128)(2,1)S(1)}, u32[]{:S(2)}, u32[]{:S(2)}) async-start(bf16[64,8,1536]{2,1,0:T(8,128)(2,1)} %bitcast.36), calls=%async_computation.3 | async-start | bytes 3145728 | tf_op jit(solution)/shard_map/all_to_all | solution.py:473
  (2 other events, 1.6 us)
where the time goes:
time: 159 us
  Pallas kernels  56.8 us (36%)
  waiting for transfers between devices  38.2 us (24%)
  blocking collectives  28.6 us (18%)
  starting transfers between devices  27.3 us (17%)
  local copies, waits for them, and re-layouts  4.25 us (3%)
  other arithmetic  1.97 us (1%)
    pallas_call x8, Pallas kernels, run(): pl.pallas_call(kernel, out_shape=outs, in_specs=[pl.BlockSpec(memory_spac...  56.8 us
    all_to_all x2, blocking collectives, exchange(): return lax.all_to_all(values, 'seq', 0, 0)  28.6 us
    all_to_all x1, waiting for transfers between devices, exchange_chips(): return lax.all_to_all(values, ('dp', 'seq'), 0, 0, axis_index_groups=CHIPS)  16.1 us
    ppermute x6, waiting for transfers between devices, shift(): lax.ppermute(values, 'seq', [(index, (index + by) % 8) for index in range...  11.8 us
    all_to_all x1, starting transfers between devices, exchange_chips(): return lax.all_to_all(values, ('dp', 'seq'), 0, 0, axis_index_groups=CHIPS)  11.2 us
    ppermute x6, waiting for transfers between devices, swap(): lax.ppermute(values, axis, [(index, index ^ bits) for index in range(size)])  10.3 us
    ppermute x6, starting transfers between devices, shift(): lax.ppermute(values, 'seq', [(index, (index + by) % 8) for index in range...  7.57 us
    ppermute x6, starting transfers between devices, swap(): lax.ppermute(values, axis, [(index, index ^ bits) for index in range(size)])  4.7 us
  transfers between devices with their start and end apart: 14, of which 12 were waited for; matrix products, arithmetic and copies ran while one was open for 2% of the time, Pallas kernels for 17%

commit v1 on v0

--- a/solution.py
+++ b/solution.py
@@ -349,8 +349,8 @@
 def sums_kernel(info_smem, *refs):
     mix, grad = refs[:2]
     pieces = refs[2 : PIECES + 2]
-    gated, up, out_w, token, mine_out = refs[PIECES + 2 : PIECES + 7]
-    others, layer, right_ref = refs[PIECES + 7 : -2], refs[-2], refs[-1]
+    gated, up, mine_out = refs[PIECES + 2 : PIECES + 5]
+    others, right_ref = refs[PIECES + 5 : -1], refs[-1]
     core = info_smem[PIECES]
     cell = TILE // 4
     mix_ref, grad_ref = mix.ready(), grad.ready()
@@ -384,8 +384,6 @@
     mine_out.send()
     for out in others[1:]:
         out.send()
-    result = dot_nn(gated_ref[...], out_w.ready()[...])
-    layer.ref[...] = (token.ready()[...].astype(F32) + result).astype(BF16)
 
 
 def join_kernel(mine, *refs):
@@ -400,7 +398,9 @@
         first += ref.shape[2]
 
 
-def input_kernel(gate_grad, grad_in, weight, token, up, out, all_grad, total):
+def input_kernel(
+    gate_grad, grad_in, weight, token, up, gated, out_w, out, layer, all_grad, total
+):
     grad_ref = grad_in.ready()
     heads = grad_ref.shape[0]
     head = grad_ref.shape[2] // 3
@@ -420,6 +420,9 @@
     second = jnp.mean(grad * normed, axis=-1, keepdims=True)
     back = (grad - first - normed * second) * inverse
     out.ref[...] = (up.ready()[...].astype(F32) + back).astype(BF16)
+    out.send()
+    result = dot_nn(gated.ready()[...], out_w.ready()[...])
+    layer.ref[...] = (token.ready()[...].astype(F32) + result).astype(BF16)
 
 
 def shift(values, by):
@@ -561,16 +564,16 @@
 
     cells = shape((8, width // 16, 4 * head + width), BF16)
     third = shape((8, width // 16, 4 * head), BF16)
-    mine, first, second, last, layer_row = call(
+    mine, first, second, last = call(
         sums_kernel,
-        [cells, third, third, third, row_shape],
+        [cells, third, third, third],
         "sums",
         smem=1,
         scratch=[pltpu.VMEM((length, 4 * head), BF16)],
-        flops=2 * length * width * 4 * head + 4 * rows * width * width,
-    )(info, mix_head, grads, *pieces, gated, upstream, out_weight, token_row)
+        flops=2 * length * width * 4 * head + 2 * rows * width * width,
+    )(info, mix_head, grads, *pieces, gated, upstream)
     others = [swap(part, "dp", 1, 16) for part in (first, second, last)]
-    both = call(join_kernel, [cells], "join", light=True)(mine, *others)[0]
+    both = call(join_kernel, [cells], "join", light=True, limit=16)(mine, *others)[0]
     both, grads_own = lax.optimization_barrier((both, grads_own))
     few = width // 128
     parts = exchange_chips(both.reshape(64, few, 4 * head + width))
@@ -579,14 +582,14 @@
     proj_out = proj_out.transpose(1, 2, 0, 3).reshape(few, 4 * width)
     out_out = jnp.sum(final[:, :, 4 * head :], axis=0)
 
-    grad_row = call(
+    grad_row, layer_row = call(
         input_kernel,
-        [shape((rows, width), BF16)],
+        [row_shape, row_shape],
         "input_grad",
         parts={2: width // TILE},
         scratch=[pltpu.VMEM((rows, 4 * width), BF16), pltpu.VMEM((rows, width), F32)],
         flops=8 * rows * width * width,
-    )(gate_grad, grads_own, proj_weight, token_row, upstream)[0]
+    )(gate_grad, grads_own, proj_weight, token_row, upstream, gated, out_weight)
     return layer_row[None], grad_row[None], proj_out, out_out
 
 

time: 159 us -> 158 us (level)
    unnamed x25 -> x21, local copies, waits for them, and re-layouts: 2.75 us -> 3.34 us
  transfers between devices with their start and end apart: 14 -> 14, of which waited for: 12 -> 12; matrix products, arithmetic and copies ran while one was open for 2% -> 2% of each run, Pallas kernels for 17% -> 16%
where the time goes in v1:
time: 158 us
  Pallas kernels  56.4 us (36%)
  waiting for transfers between devices  37 us (23%)
  blocking collectives  28.6 us (18%)
  starting transfers between devices  27.3 us (17%)
  local copies, waits for them, and re-layouts  4.86 us (3%)
  other arithmetic  1.97 us (1%)
    pallas_call x8, Pallas kernels, run(): pl.pallas_call(kernel, out_shape=outs, in_specs=[pl.BlockSpec(memory_spac...  56.4 us
    all_to_all x2, blocking collectives, exchange(): return lax.all_to_all(values, 'seq', 0, 0)  28.6 us
    all_to_all x1, waiting for transfers between devices, exchange_chips(): return lax.all_to_all(values, ('dp', 'seq'), 0, 0, axis_index_groups=CHIPS)  14.9 us
    ppermute x6, waiting for transfers between devices, shift(): lax.ppermute(values, 'seq', [(index, (index + by) % 8) for index in range...  11.8 us
    all_to_all x1, starting transfers between devices, exchange_chips(): return lax.all_to_all(values, ('dp', 'seq'), 0, 0, axis_index_groups=CHIPS)  11.2 us
    ppermute x6, waiting for transfers between devices, swap(): lax.ppermute(values, axis, [(index, index ^ bits) for index in range(size)])  10.3 us
    ppermute x6, starting transfers between devices, shift(): lax.ppermute(values, 'seq', [(index, (index + by) % 8) for index in range...  7.57 us
    ppermute x6, starting transfers between devices, swap(): lax.ppermute(values, axis, [(index, index ^ bits) for index in range(size)])  4.7 us
  transfers between devices with their start and end apart: 14, of which 12 were waited for; matrix products, arithmetic and copies ran while one was open for 2% of the time, Pallas kernels for 16%

profile of v1, /device:TPU:0, one launch (start us, length us, event | category | flops | bytes accessed | tf_op | source)
XLA Modules:
  0.0 157.8 jit_solution(1344713615816113266)
XLA Ops:
  0.6 2.2 %norm.1.refs_2_.refs_4_.refs_3_ = bf16[256,1024]{1,0:T(8,128)(2,1)} custom-call(bf16[256,1024]{1,0:T(8,128)(2,1)} %bitcast.40), custom_call_target="tpu_custom_call" | custom-call | bytes 1048576 | tf_op jit(solution)/shard_map/norm/pallas_call | solution.py:128
  2.8 1.6 %collective-permute-start.2 = (bf16[256,1024]{1,0:T(8,128)(2,1)}, bf16[256,1024]{1,0:T(8,128)(2,1)S(1)}, u32[]{:S(2)}, u32[]{:S(2)}) collective-permute-start(bf16[256,1024]{1,0:T(8,128)(2,1)} %norm.1.refs_2_.refs_4_.refs_3_), channel_id=1, source_target_pairs={{0,2},{1,3},{2,4},{3,5},{4,6},{5,7},{6,0},{7,1},{8,10},{9,11},{10,... | collective-permute-start | bytes 1572872 | tf_op jit(solution)/shard_map/ppermute | solution.py:429
  4.5 1.7 %collective-permute-start.1 = (bf16[256,1024]{1,0:T(8,128)(2,1)}, bf16[256,1024]{1,0:T(8,128)(2,1)S(1)}, u32[]{:S(2)}, u32[]{:S(2)}) collective-permute-start(bf16[256,1024]{1,0:T(8,128)(2,1)} %norm.1.refs_2_.refs_4_.refs_3_), channel_id=1, source_target_pairs={{0,6},{1,7},{2,0},{3,1},{4,2},{5,3},{6,4},{7,5},{8,14},{9,15},{10,... | collective-permute-start | bytes 1572872 | tf_op jit(solution)/shard_map/ppermute | solution.py:429
  6.1 2.0 %collective-permute-start = (bf16[256,1024]{1,0:T(8,128)(2,1)}, bf16[256,1024]{1,0:T(8,128)(2,1)S(1)}, u32[]{:S(2)}, u32[]{:S(2)}) collective-permute-start(bf16[256,1024]{1,0:T(8,128)(2,1)} %norm.1.refs_2_.refs_4_.refs_3_), channel_id=1, source_target_pairs={{0,1},{1,0},{2,3},{3,2},{4,5},{5,4},{6,7},{7,6},{8,9},{9,8},{10,11... | collective-permute-start | bytes 1572872 | tf_op jit(solution)/shard_map/ppermute | solution.py:433
  9.7 5.6 %prepare.1 = (f32[256,1024]{1,0:T(8,128)}, f32[256,1024]{1,0:T(8,128)}, bf16[1024,384]{1,0:T(8,128)(2,1)}) custom-call(s32[1]{0:T(128)} %bitcast.12.refs_0_, bf16[256,1024]{1,0:T(8,128)(2,1)} %bitcast.37, bf16[256,1024]{1,0:T(8,128)(2,1)} %norm.1.refs_2_.refs_4_.refs_3_, bf16[1024,1024]{1,0:T(8,128)(2,1)} %refs_6_.1, bf16[1024,4096]{1,0:T(8,128)(2,1)} %refs_2_.1), custom_call_target="tpu_custom_call" | custom-call | flops 1073741824 | bytes 14417924 | tf_op jit(solution)/shard_map/prepare/pallas_call | solution.py:128
  18.1 1.7 %collective-permute-done.refs_5_.refs_4_ = bf16[256,1024]{1,0:T(8,128)(2,1)S(1)} collective-permute-done((bf16[256,1024]{1,0:T(8,128)(2,1)}, bf16[256,1024]{1,0:T(8,128)(2,1)S(1)}, u32[]{:S(2)}, u32[]{:S(2)}) %collective-permute-start) | collective-permute-done | bytes 524320 | tf_op jit(solution)/shard_map/ppermute | solution.py:433
  19.7 1.7 %collective-permute-start.5 = (bf16[256,1024]{1,0:T(8,128)(2,1)S(1)}, bf16[256,1024]{1,0:T(8,128)(2,1)S(1)}, u32[]{:S(2)}, u32[]{:S(2)}) collective-permute-start(bf16[256,1024]{1,0:T(8,128)(2,1)S(1)} %collective-permute-done.2.refs_7_.refs_6_), channel_id=1, source_target_pairs={{0,1},{1,0},{2,3},{3,2},{4,5},{5,4},{6,7},{7,6},{8,9},{9,8},{10,11... | collective-permute-start | bytes 1572872 | tf_op jit(solution)/shard_map/ppermute | solution.py:433
  21.5 1.6 %collective-permute-start.3 = (bf16[128,1024]{1,0:T(8,128)(2,1)S(1)}, bf16[128,1024]{1,0:T(8,128)(2,1)S(1)}, u32[]{:S(2)}, u32[]{:S(2)}) collective-permute-start(bf16[128,1024]{1,0:T(8,128)(2,1)S(1)} %slice.19), channel_id=1, source_target_pairs={{0,6},{1,7},{2,0},{3,1},{4,2},{5,3},{6,4},{7,5},{8,14},{9,15},{10,... | collective-permute-start | bytes 786440 | tf_op jit(solution)/shard_map/ppermute | solution.py:429
  25.2 5.6 %collective-permute-done.3.refs_8_.refs_7_ = bf16[128,1024]{1,0:T(8,128)(2,1)S(1)} collective-permute-done((bf16[128,1024]{1,0:T(8,128)(2,1)S(1)}, bf16[128,1024]{1,0:T(8,128)(2,1)S(1)}, u32[]{:S(2)}, u32[]{:S(2)}) %collective-permute-start.3) | collective-permute-done | bytes 262176 | tf_op jit(solution)/shard_map/ppermute | solution.py:429
  31.1 3.5 %collective-permute-done.5.refs_10_.refs_9_ = bf16[256,1024]{1,0:T(8,128)(2,1)S(1)} collective-permute-done((bf16[256,1024]{1,0:T(8,128)(2,1)S(1)}, bf16[256,1024]{1,0:T(8,128)(2,1)S(1)}, u32[]{:S(2)}, u32[]{:S(2)}) %collective-permute-start.5) | collective-permute-done | bytes 524320 | tf_op jit(solution)/shard_map/ppermute | solution.py:433
  35.8 2.1 %collective-permute-done.7.refs_12_.refs_11_ = bf16[128,1024]{1,0:T(8,128)(2,1)} collective-permute-done((bf16[128,1024]{1,0:T(8,128)(2,1)S(1)}, bf16[128,1024]{1,0:T(8,128)(2,1)}, u32[]{:S(2)}, u32[]{:S(2)}) %collective-permute-start.7) | collective-permute-done | bytes 262176 | tf_op jit(solution)/shard_map/ppermute | solution.py:433
  39.0 3.5 %collective-permute-done.8.refs_13_.refs_12_ = bf16[128,1024]{1,0:T(8,128)(2,1)} collective-permute-done((bf16[128,1024]{1,0:T(8,128)(2,1)S(1)}, bf16[128,1024]{1,0:T(8,128)(2,1)}, u32[]{:S(2)}, u32[]{:S(2)}) %collective-permute-start.8) | collective-permute-done | bytes 262176 | tf_op jit(solution)/shard_map/ppermute | solution.py:429
  42.6 11.5 %forward.1 = (bf16[2048,384]{1,0:T(8,128)(2,1)}, bf16[2048,384]{1,0:T(8,128)(2,1)}, bf16[8,272,128]{2,1,0:T(8,128)(2,1)}) custom-call(s32[11]{0:T(128)} %stack.47.refs_0_, bf16[1024,384]{1,0:T(8,128)(2,1)} %get-tuple-element.32.refs_1_, f32[1,1024]{1,0:T(1,128)} %fusion.1.refs_2_.refs_0_, bf16[2048,128]{1,0:T(8,128)(2,1)} %fusion.refs_3_.refs_1_, ...), custom_call_target="tpu_custom_call" | custom-call | flops 2147483648 | bytes 9211948 | tf_op jit(solution)/shard_map/forward/pallas_call | solution.py:128
  54.1 13.2 %all_to_all.20.refs_0_ = bf16[8,272,128]{2,1,0:T(8,128)(2,1)} all-to-all(bf16[8,272,128]{2,1,0:T(8,128)(2,1)} %get-tuple-element.38), channel_id=1, replica_groups=mesh['dp'=16,'seq'=8] {'seq'}, dimensions={0} | all-to-all | bytes 1114112 | tf_op jit(solution)/shard_map/all_to_all | solution.py:480
  67.3 4.3 %mix.1 = (bf16[8,256,256]{2,1,0:T(8,128)(2,1)}, bf16[256,1024]{1,0:T(8,128)(2,1)}, bf16[256,1024]{1,0:T(8,128)(2,1)}) custom-call(bf16[8,272,128]{2,1,0:T(8,128)(2,1)} %all_to_all.20.refs_0_, f32[256,1024]{1,0:T(8,128)} %get-tuple-element.39.refs_1_, f32[256,1024]{1,0:T(8,128)} %get-tuple-element.40.refs_2_), custom_call_target="tpu_custom_call" | custom-call | bytes 4751360 | tf_op jit(solution)/shard_map/mix/pallas_call | solution.py:128
  71.6 15.4 %all_to_all.21.refs_3_.refs_1_ = bf16[8,256,256]{2,1,0:T(8,128)(2,1)} all-to-all(bf16[8,256,256]{2,1,0:T(8,128)(2,1)} %get-tuple-element.42), channel_id=1, replica_groups=mesh['dp'=16,'seq'=8] {'seq'}, dimensions={0} | all-to-all | bytes 2097152 | tf_op jit(solution)/shard_map/all_to_all | solution.py:480
  86.9 12.4 %backward.1.refs_2_ = bf16[8,256,384]{2,1,0:T(8,128)(2,1)} custom-call(f32[1,1024]{1,0:T(1,128)} %fusion.1.refs_2_.refs_0_, bf16[2048,128]{1,0:T(8,128)(2,1)} %fusion.refs_3_.refs_1_, bf16[2048,384]{1,0:T(8,128)(2,1)} %get-tuple-element.43.refs_2_, bf16[8,256,256]{2,1,0:T(8,128)(2,1)} %all_to_all.21.refs_3_.refs_1_, bf16[2048,384]{1,0:T(8,128)(2,1)} %get-tuple-element.44.refs_4_), custom_call_target="tpu_custom_call" | custom-call | flops 10737418240 | bytes 6295552 | tf_op jit(solution)/shard_map/backward/pallas_call | solution.py:128
  99.4 3.9 %all-to-all-start.2 = ((bf16[8,256,384]{2,1,0:T(8,128)(2,1)}), bf16[8,256,384]{2,1,0:T(8,128)(2,1)S(1)}, u32[]{:S(2)}, u32[]{:S(2)}) async-start(bf16[8,256,384]{2,1,0:T(8,128)(2,1)} %backward.1.refs_2_), calls=%async_computation.2 | async-start | bytes 3145728 | tf_op jit(solution)/shard_map/all_to_all | solution.py:480
  103.3 8.7 %sums.1 = (bf16[8,64,1536]{2,1,0:T(8,128)(2,1)}, bf16[8,64,512]{2,1,0:T(8,128)(2,1)}, bf16[8,64,512]{2,1,0:T(8,128)(2,1)}, bf16[8,64,512]{2,1,0:T(8,128)(2,1)}) custom-call(s32[11]{0:T(128)} %stack.47.refs_0_, bf16[8,256,256]{2,1,0:T(8,128)(2,1)} %all_to_all.21.refs_3_.refs_1_, bf16[8,256,384]{2,1,0:T(8,128)(2,1)} %backward.1.refs_2_, ...), custom_call_target="tpu_custom_call" | custom-call | flops 2684354560 | bytes 11010092 | tf_op jit(solution)/shard_map/sums/pallas_call | solution.py:128
  112.6 1.5 collective-permute-done.9.refs_1_
  117.0 1.8 %join.1 = bf16[8,64,1536]{2,1,0:T(8,128)(2,1)} custom-call(bf16[8,64,1536]{2,1,0:T(8,128)(2,1)S(1)} %copy-done.1, bf16[8,64,512]{2,1,0:T(8,128)(2,1)S(1)} %collective-permute-done.9.refs_1_, bf16[8,64,512]{2,1,0:T(8,128)(2,1)S(1)} %collective-permute-done.10.refs_2_, bf16[8,64,512]{2,1,0:T(8,128)(2,1)S(1)} %collective-permute-done.11.refs_3_), custom_call_target="tpu_custom_call" | custom-call | tf_op jit(solution)/shard_map/join/pallas_call | solution.py:128
  120.0 11.2 %all-to-all-start.3 = ((bf16[64,8,1536]{2,1,0:T(8,128)(2,1)}), bf16[64,8,1536]{2,1,0:T(8,128)(2,1)S(1)}, u32[]{:S(2)}, u32[]{:S(2)}) async-start(bf16[64,8,1536]{2,1,0:T(8,128)(2,1)} %bitcast.20), calls=%async_computation.3 | async-start | bytes 3145728 | tf_op jit(solution)/shard_map/all_to_all | solution.py:476
  131.2 10.0 %input_grad.1 = (bf16[256,1024]{1,0:T(8,128)(2,1)}, bf16[256,1024]{1,0:T(8,128)(2,1)}) custom-call(bf16[256,1024]{1,0:T(8,128)(2,1)} %get-tuple-element.41.refs_0_, bf16[8,256,384]{2,1,0:T(8,128)(2,1)} %copy-done.2, bf16[1024,4096]{1,0:T(8,128)(2,1)} %refs_2_.1, bf16[256,1024]{1,0:T(8,128)(2,1)} %bitcast.41, bf16[256,1024]{1,0:T(8,128)(2,1)} %bitcast.39, ...), custom_call_target="tpu_custom_call" | custom-call | flops 2147483648 | bytes 15204352 | tf_op jit(solution)/shard_map/input_grad/pallas_call | solution.py:128
  141.2 14.9 %all-to-all-done.3 = bf16[64,8,1536]{2,1,0:T(8,128)(2,1)S(1)} async-done(((bf16[64,8,1536]{2,1,0:T(8,128)(2,1)}), bf16[64,8,1536]{2,1,0:T(8,128)(2,1)S(1)}, u32[]{:S(2)}, u32[]{:S(2)}) %all-to-all-start.3) | async-done | bytes 1572896 | tf_op jit(solution)/shard_map/all_to_all | solution.py:476
  (46 shorter events, 15.6 us)
Async XLA Ops:
  0.6 8.2 %copy-start = (f32[8,128]{1,0:T(8,128)S(1)}, f32[8,128]{1,0:T(8,128)}, u32[]{:S(2)}) copy-start(f32[8,128]{1,0:T(8,128)} %param.10) | copy-start | bytes 12292
  2.8 15.0 %collective-permute-start.2 = (bf16[256,1024]{1,0:T(8,128)(2,1)}, bf16[256,1024]{1,0:T(8,128)(2,1)S(1)}, u32[]{:S(2)}, u32[]{:S(2)}) collective-permute-start(bf16[256,1024]{1,0:T(8,128)(2,1)} %norm.1.refs_2_.refs_4_.refs_3_), channel_id=1, source_target_pairs={{0,2},{1,3},{2,4},{3,5},{4,6},{5,7},{6,0},{7,1},{8,10},{9,11},{10,... | collective-permute-start | bytes 1572872 | tf_op jit(solution)/shard_map/ppermute | solution.py:429
  4.5 13.6 %collective-permute-start.1 = (bf16[256,1024]{1,0:T(8,128)(2,1)}, bf16[256,1024]{1,0:T(8,128)(2,1)S(1)}, u32[]{:S(2)}, u32[]{:S(2)}) collective-permute-start(bf16[256,1024]{1,0:T(8,128)(2,1)} %norm.1.refs_2_.refs_4_.refs_3_), channel_id=1, source_target_pairs={{0,6},{1,7},{2,0},{3,1},{4,2},{5,3},{6,4},{7,5},{8,14},{9,15},{10,... | collective-permute-start | bytes 1572872 | tf_op jit(solution)/shard_map/ppermute | solution.py:429
  6.1 13.6 %collective-permute-start = (bf16[256,1024]{1,0:T(8,128)(2,1)}, bf16[256,1024]{1,0:T(8,128)(2,1)S(1)}, u32[]{:S(2)}, u32[]{:S(2)}) collective-permute-start(bf16[256,1024]{1,0:T(8,128)(2,1)} %norm.1.refs_2_.refs_4_.refs_3_), channel_id=1, source_target_pairs={{0,1},{1,0},{2,3},{3,2},{4,5},{5,4},{6,7},{7,6},{8,9},{9,8},{10,11... | collective-permute-start | bytes 1572872 | tf_op jit(solution)/shard_map/ppermute | solution.py:433
  9.7 5.6 %copy-start.6 = (s32[1,2048]{1,0:T(1,128)S(1)}, s32[1,2048]{1,0:T(1,128)}, u32[]{:S(2)}) copy-start(s32[1,2048]{1,0:T(1,128)} %param.11) | copy-start | bytes 24580
  17.9 24.7 %copy-start.3 = (bf16[256,1024]{1,0:T(8,128)(2,1)}, bf16[256,1024]{1,0:T(8,128)(2,1)S(1)}, u32[]{:S(2)}) copy-start(bf16[256,1024]{1,0:T(8,128)(2,1)S(1)} %collective-permute-done.2.refs_7_.refs_6_) | copy-start | bytes 1572868
  18.1 24.5 %copy-start.4 = (bf16[256,1024]{1,0:T(8,128)(2,1)}, bf16[256,1024]{1,0:T(8,128)(2,1)S(1)}, u32[]{:S(2)}) copy-start(bf16[256,1024]{1,0:T(8,128)(2,1)S(1)} %collective-permute-done.1.refs_6_.refs_5_) | copy-start | bytes 1572868
  19.7 22.8 %copy-start.7 = (bf16[256,1024]{1,0:T(8,128)(2,1)}, bf16[256,1024]{1,0:T(8,128)(2,1)S(1)}, u32[]{:S(2)}) copy-start(bf16[256,1024]{1,0:T(8,128)(2,1)S(1)} %collective-permute-done.refs_5_.refs_4_) | copy-start | bytes 1572868
  19.7 14.9 %collective-permute-start.5 = (bf16[256,1024]{1,0:T(8,128)(2,1)S(1)}, bf16[256,1024]{1,0:T(8,128)(2,1)S(1)}, u32[]{:S(2)}, u32[]{:S(2)}) collective-permute-start(bf16[256,1024]{1,0:T(8,128)(2,1)S(1)} %collective-permute-done.2.refs_7_.refs_6_), channel_id=1, source_target_pairs={{0,1},{1,0},{2,3},{3,2},{4,5},{5,4},{6,7},{7,6},{8,9},{9,8},{10,11... | collective-permute-start | bytes 1572872 | tf_op jit(solution)/shard_map/ppermute | solution.py:433
  21.5 9.3 %collective-permute-start.3 = (bf16[128,1024]{1,0:T(8,128)(2,1)S(1)}, bf16[128,1024]{1,0:T(8,128)(2,1)S(1)}, u32[]{:S(2)}, u32[]{:S(2)}) collective-permute-start(bf16[128,1024]{1,0:T(8,128)(2,1)S(1)} %slice.19), channel_id=1, source_target_pairs={{0,6},{1,7},{2,0},{3,1},{4,2},{5,3},{6,4},{7,5},{8,14},{9,15},{10,... | collective-permute-start | bytes 786440 | tf_op jit(solution)/shard_map/ppermute | solution.py:429
  23.1 15.9 %collective-permute-start.6 = (bf16[256,1024]{1,0:T(8,128)(2,1)S(1)}, bf16[256,1024]{1,0:T(8,128)(2,1)S(1)}, u32[]{:S(2)}, u32[]{:S(2)}) collective-permute-start(bf16[256,1024]{1,0:T(8,128)(2,1)S(1)} %collective-permute-done.refs_5_.refs_4_), channel_id=1, source_target_pairs={{0,6},{1,7},{2,0},{3,1},{4,2},{5,3},{6,4},{7,5},{8,14},{9,15},{10,... | collective-permute-start | bytes 1572872 | tf_op jit(solution)/shard_map/ppermute | solution.py:429
  23.9 11.9 %collective-permute-start.4 = (bf16[128,1024]{1,0:T(8,128)(2,1)S(1)}, bf16[128,1024]{1,0:T(8,128)(2,1)}, u32[]{:S(2)}, u32[]{:S(2)}) collective-permute-start(bf16[128,1024]{1,0:T(8,128)(2,1)S(1)} %slice.20), channel_id=1, source_target_pairs={{0,2},{1,3},{2,4},{3,5},{4,6},{5,7},{6,0},{7,1},{8,10},{9,11},{10,... | collective-permute-start | bytes 786440 | tf_op jit(solution)/shard_map/ppermute | solution.py:429
  30.8 11.8 %copy-start.9 = (bf16[128,1024]{1,0:T(8,128)(2,1)}, bf16[128,1024]{1,0:T(8,128)(2,1)S(1)}, u32[]{:S(2)}) copy-start(bf16[128,1024]{1,0:T(8,128)(2,1)S(1)} %collective-permute-done.3.refs_8_.refs_7_) | copy-start | bytes 786436
  30.8 7.2 %collective-permute-start.7 = (bf16[128,1024]{1,0:T(8,128)(2,1)S(1)}, bf16[128,1024]{1,0:T(8,128)(2,1)}, u32[]{:S(2)}, u32[]{:S(2)}) collective-permute-start(bf16[128,1024]{1,0:T(8,128)(2,1)S(1)} %collective-permute-done.3.refs_8_.refs_7_), channel_id=1, source_target_pairs={{0,1},{1,0},{2,3},{3,2},{4,5},{5,4},{6,7},{7,6},{8,9},{9,8},{10,11... | collective-permute-start | bytes 786440 | tf_op jit(solution)/shard_map/ppermute | solution.py:433
  34.6 8.0 %copy-start.5 = (bf16[256,1024]{1,0:T(8,128)(2,1)}, bf16[256,1024]{1,0:T(8,128)(2,1)S(1)}, u32[]{:S(2)}) copy-start(bf16[256,1024]{1,0:T(8,128)(2,1)S(1)} %collective-permute-done.5.refs_10_.refs_9_) | copy-start | bytes 1572868
  34.6 7.9 %collective-permute-start.8 = (bf16[128,1024]{1,0:T(8,128)(2,1)S(1)}, bf16[128,1024]{1,0:T(8,128)(2,1)}, u32[]{:S(2)}, u32[]{:S(2)}) collective-permute-start(bf16[128,1024]{1,0:T(8,128)(2,1)S(1)} %slice.24), channel_id=1, source_target_pairs={{0,2},{1,3},{2,4},{3,5},{4,6},{5,7},{6,0},{7,1},{8,10},{9,11},{10,... | collective-permute-start | bytes 786440 | tf_op jit(solution)/shard_map/ppermute | solution.py:429
  39.0 3.5 %copy-start.8 = (bf16[256,1024]{1,0:T(8,128)(2,1)}, bf16[256,1024]{1,0:T(8,128)(2,1)S(1)}, u32[]{:S(2)}) copy-start(bf16[256,1024]{1,0:T(8,128)(2,1)S(1)} %collective-permute-done.6.refs_11_.refs_10_) | copy-start | bytes 1572868
  99.4 19.4 %all-to-all-start.2 = ((bf16[8,256,384]{2,1,0:T(8,128)(2,1)}), bf16[8,256,384]{2,1,0:T(8,128)(2,1)S(1)}, u32[]{:S(2)}, u32[]{:S(2)}) async-start(bf16[8,256,384]{2,1,0:T(8,128)(2,1)} %backward.1.refs_2_), calls=%async_computation.2 | async-start | bytes 3145728 | tf_op jit(solution)/shard_map/all_to_all | solution.py:480
  111.9 2.2 %collective-permute-start.9 = (bf16[8,64,512]{2,1,0:T(8,128)(2,1)}, bf16[8,64,512]{2,1,0:T(8,128)(2,1)S(1)}, u32[]{:S(2)}, u32[]{:S(2)}) collective-permute-start(bf16[8,64,512]{2,1,0:T(8,128)(2,1)} %get-tuple-element.47), channel_id=1, source_target_pairs={{0,8},{8,0},{16,24},{24,16},{32,40},{40,32},{48,56},{56,48},{64,72... | collective-permute-start | bytes 1572872 | tf_op jit(solution)/shard_map/ppermute | solution.py:433
  112.0 2.9 %collective-permute-start.10 = (bf16[8,64,512]{2,1,0:T(8,128)(2,1)}, bf16[8,64,512]{2,1,0:T(8,128)(2,1)S(1)}, u32[]{:S(2)}, u32[]{:S(2)}) collective-permute-start(bf16[8,64,512]{2,1,0:T(8,128)(2,1)} %get-tuple-element.48), channel_id=1, source_target_pairs={{0,8},{8,0},{16,24},{24,16},{32,40},{40,32},{48,56},{56,48},{64,72... | collective-permute-start | bytes 1572872 | tf_op jit(solution)/shard_map/ppermute | solution.py:433
  112.5 3.1 %collective-permute-start.11 = (bf16[8,64,512]{2,1,0:T(8,128)(2,1)}, bf16[8,64,512]{2,1,0:T(8,128)(2,1)S(1)}, u32[]{:S(2)}, u32[]{:S(2)}) collective-permute-start(bf16[8,64,512]{2,1,0:T(8,128)(2,1)} %get-tuple-element.49), channel_id=1, source_target_pairs={{0,8},{8,0},{16,24},{24,16},{32,40},{40,32},{48,56},{56,48},{64,72... | collective-permute-start | bytes 1572872 | tf_op jit(solution)/shard_map/ppermute | solution.py:433
  115.6 1.4 copy-start.1
  118.8 1.2 copy-start.2
  120.0 36.1 %all-to-all-start.3 = ((bf16[64,8,1536]{2,1,0:T(8,128)(2,1)}), bf16[64,8,1536]{2,1,0:T(8,128)(2,1)S(1)}, u32[]{:S(2)}, u32[]{:S(2)}) async-start(bf16[64,8,1536]{2,1,0:T(8,128)(2,1)} %bitcast.20), calls=%async_computation.3 | async-start | bytes 3145728 | tf_op jit(solution)/shard_map/all_to_all | solution.py:476

commit v2 on v1

--- a/solution.py
+++ b/solution.py
@@ -197,13 +197,41 @@
     return ((1.0 - mask.astype(F32)) * DEAD).astype(BF16)
 
 
+def project(values, weight):
+    half = 0.5 * dot_nn(values, weight)
+    lean = jnp.tanh(half)
+    rise = 1.0 + lean
+    slope = 0.5 * rise * (1.0 + half * (1.0 - lean))
+    return (half * rise).astype(BF16), slope.astype(BF16)
+
+
+def early_kernel(weight, *refs):
+    pieces, (feature, slope) = refs[:EARLY], refs[EARLY:]
+    weight_ref = weight.ready()
+    for index, piece in enumerate(pieces):
+        rows = slice(index * TILE, (index + 1) * TILE)
+        made, rate = project(piece.ready()[...], weight_ref[...])
+        feature.ref[rows, :] = made
+        slope.ref[rows, :] = rate
+
+
 def forward_kernel(scale, start_smem, *refs):
-    weight, table, mask = refs[:3]
-    pieces = refs[3 : PIECES + 3]
-    feature, slope, attended, bias_ref, key_ref = refs[PIECES + 3 :]
+    weight, table, mask, feature_early, slope_early = refs[:5]
+    pieces = refs[5 : PIECES - EARLY + 5]
+    feature, slope, attended, bias_ref, key_ref, sems = refs[PIECES - EARLY + 5 :]
     feature_ref, slope_ref = feature.ref, slope.ref
     count, _, head = attended.ref.shape
     reach = bias_ref.shape[0] - 1
+    copies = []
+    for index in range(EARLY):
+        source = pl.ds(index * TILE, TILE)
+        rows = pl.ds(pl.multiple_of(start_smem[index], HALF), TILE)
+        for far, near in ((feature_early, feature_ref), (slope_early, slope_ref)):
+            copies.append(
+                pltpu.make_async_copy(far.at[source], near.at[rows], sems.at[len(copies)])
+            )
+    for copy in copies:
+        copy.start()
     row_at = lax.broadcasted_iota(jnp.int32, (16, HALF), 0)
     bias_tiles(table.ready(), bias_ref, False)
     mask_ref = mask.ready()
@@ -211,16 +239,15 @@
     weight_ref = weight.ready()
     for index, piece in enumerate(pieces):
         ref = piece.ready()
-        rows = pl.ds(pl.multiple_of(start_smem[index], HALF), ref.shape[0])
-        half = 0.5 * dot_nn(ref[...], weight_ref[...])
-        lean = jnp.tanh(half)
-        rise = 1.0 + lean
-        made = (half * rise).astype(BF16)
+        rows = pl.ds(pl.multiple_of(start_smem[index + EARLY], HALF), ref.shape[0])
+        made, rate = project(ref[...], weight_ref[...])
         feature_ref[rows, :] = made
-        key_ref[rows, :head] = made[:, 2 * head :]
-        slope_ref[rows, :] = (0.5 * rise * (1.0 + half * (1.0 - lean))).astype(BF16)
+        slope_ref[rows, :] = rate
+    for copy in copies:
+        copy.wait()
     feature.send()
     slope.send()
+    key_ref[:, :head] = feature_ref[:, 2 * head :]
     for q_block in range(count):
         rows = slice(q_block * TILE, (q_block + 1) * TILE)
         query = jnp.concatenate([feature_ref[rows, head : 2 * head], mask_ref[rows, :]], axis=1)
@@ -437,11 +464,12 @@
     return swap(own, "seq", 1, 8), shift(own, -2), shift(own, 2)
 
 
-def gather_rest(own, mate, after, before):
+def gather_rest(own, mate, after, before, early):
     half = own.shape[0] // 2
     across_low = shift(after[:half], -2)
     across_high = shift(before[half:], 2)
     mate_before = swap(before, "seq", 1, 8)
+    mate_before, early = lax.optimization_barrier((mate_before, early))
     mate_after = shift(mate, -2)
     mate_across_low = swap(across_low, "seq", 1, 8)
     mate_across_high = shift(mate_before[half:], 2)
@@ -460,10 +488,11 @@
         (mate_across_high, other + 4, half),
     ]
     starts = [(place % 8) * own.shape[0] + first for _, place, first in pieces]
-    return [piece for piece, _, _ in pieces], starts
+    return [piece for piece, _, _ in pieces], starts, early
 
 
 PIECES = 10
+EARLY = 4
 HALF = TILE // 2
 
 
@@ -519,7 +548,9 @@
     near, gg, gate_proj, weight, table, mask = lax.optimization_barrier(
         (near, gg, gate_proj, weight, table, mask)
     )
-    pieces, starts = gather_rest(half, *near)
+    kept = shape((EARLY * rows, 3 * head), BF16)
+    early = call(early_kernel, [kept, kept], "early", light=True)(weight, half, *near)
+    pieces, starts, early = gather_rest(half, *near, early)
     info = lax.optimization_barrier(jnp.stack(starts + [core]))
 
     tiles = pltpu.VMEM((reach + 1, TILE, TILE), F32)
@@ -533,9 +564,12 @@
         "forward",
         smem=1,
         out_parts={2: 8},
-        scratch=[tiles, pltpu.VMEM((length, 2 * head), BF16)],
+        far=(4, 5),
+        scratch=[
+            tiles, pltpu.VMEM((length, 2 * head), BF16), pltpu.SemaphoreType.DMA((2 * EARLY,))
+        ],
         flops=2 * length * width * 4 * head,
-    )(info, weight, table, mask, *pieces)
+    )(info, weight, table, mask, *early, *pieces[EARLY:])
     attended_own = exchange(attended)
 
     row_shape = shape((rows, width), BF16)

time: 158 us -> 156 us (0.987)
  waiting for transfers between devices: 37 us -> 32.1 us
  Pallas kernels: 56.4 us -> 58.9 us
    ppermute x6, waiting for transfers between devices: 11.8 us -> 6.93 us  [shift(): lax.ppermute(values, 'seq', [(index, (index + by) % 8) for index in range...]
    pallas_call x8 -> x9, Pallas kernels: 56.4 us -> 58.9 us  [run(): pl.pallas_call(kernel, out_shape=outs, in_specs=[pl.BlockSpec(memory_spac...]
    unnamed x21 -> x25, local copies, waits for them, and re-layouts: 3.34 us -> 4.03 us
  transfers between devices with their start and end apart: 14 -> 14, of which waited for: 12 -> 12; matrix products, arithmetic and copies ran while one was open for 2% -> 2% of each run, Pallas kernels for 16% -> 20%
where the time goes in v2:
time: 156 us; the launch traced here: 155 us
  Pallas kernels  58.9 us (38%)
  waiting for transfers between devices  32.1 us (21%)
  blocking collectives  28.6 us (18%)
  starting transfers between devices  26.6 us (17%)
  local copies, waits for them, and re-layouts  5.54 us (4%)
  other arithmetic  1.97 us (1%)
    pallas_call x9, Pallas kernels, run(): pl.pallas_call(kernel, out_shape=outs, in_specs=[pl.BlockSpec(memory_spac...  58.9 us
    all_to_all x2, blocking collectives, exchange(): return lax.all_to_all(values, 'seq', 0, 0)  28.6 us
    all_to_all x1, waiting for transfers between devices, exchange_chips(): return lax.all_to_all(values, ('dp', 'seq'), 0, 0, axis_index_groups=CHIPS)  14.9 us
    all_to_all x1, starting transfers between devices, exchange_chips(): return lax.all_to_all(values, ('dp', 'seq'), 0, 0, axis_index_groups=CHIPS)  10.7 us
    ppermute x6, waiting for transfers between devices, swap(): lax.ppermute(values, axis, [(index, index ^ bits) for index in range(size)])  10.3 us
    ppermute x6, starting transfers between devices, shift(): lax.ppermute(values, 'seq', [(index, (index + by) % 8) for index in range...  7.35 us
    ppermute x6, waiting for transfers between devices, shift(): lax.ppermute(values, 'seq', [(index, (index + by) % 8) for index in range...  6.93 us
    ppermute x6, starting transfers between devices, swap(): lax.ppermute(values, axis, [(index, index ^ bits) for index in range(size)])  4.7 us
  transfers between devices with their start and end apart: 14, of which 12 were waited for; matrix products, arithmetic and copies ran while one was open for 2% of the time, Pallas kernels for 20%

profile of v2, /device:TPU:0, one launch (start us, length us, event | category | flops | bytes accessed | tf_op | source)
XLA Modules:
  0.0 155.5 jit_solution(8359808784720323190)
XLA Ops:
  0.6 2.2 %norm.1.refs_2_.refs_1_.refs_3_ = bf16[256,1024]{1,0:T(8,128)(2,1)} custom-call(bf16[256,1024]{1,0:T(8,128)(2,1)} %bitcast.40), custom_call_target="tpu_custom_call" | custom-call | bytes 1048576 | tf_op jit(solution)/shard_map/norm/pallas_call | solution.py:128
  2.8 1.6 %collective-permute-start.2 = (bf16[256,1024]{1,0:T(8,128)(2,1)}, bf16[256,1024]{1,0:T(8,128)(2,1)S(1)}, u32[]{:S(2)}, u32[]{:S(2)}) collective-permute-start(bf16[256,1024]{1,0:T(8,128)(2,1)} %norm.1.refs_2_.refs_1_.refs_3_), channel_id=1, source_target_pairs={{0,2},{1,3},{2,4},{3,5},{4,6},{5,7},{6,0},{7,1},{8,10},{9,11},{10,... | collective-permute-start | bytes 1572872 | tf_op jit(solution)/shard_map/ppermute | solution.py:456
  4.5 1.7 %collective-permute-start.1 = (bf16[256,1024]{1,0:T(8,128)(2,1)}, bf16[256,1024]{1,0:T(8,128)(2,1)S(1)}, u32[]{:S(2)}, u32[]{:S(2)}) collective-permute-start(bf16[256,1024]{1,0:T(8,128)(2,1)} %norm.1.refs_2_.refs_1_.refs_3_), channel_id=1, source_target_pairs={{0,6},{1,7},{2,0},{3,1},{4,2},{5,3},{6,4},{7,5},{8,14},{9,15},{10,... | collective-permute-start | bytes 1572872 | tf_op jit(solution)/shard_map/ppermute | solution.py:456
  6.1 2.0 %collective-permute-start = (bf16[256,1024]{1,0:T(8,128)(2,1)}, bf16[256,1024]{1,0:T(8,128)(2,1)S(1)}, u32[]{:S(2)}, u32[]{:S(2)}) collective-permute-start(bf16[256,1024]{1,0:T(8,128)(2,1)} %norm.1.refs_2_.refs_1_.refs_3_), channel_id=1, source_target_pairs={{0,1},{1,0},{2,3},{3,2},{4,5},{5,4},{6,7},{7,6},{8,9},{9,8},{10,11... | collective-permute-start | bytes 1572872 | tf_op jit(solution)/shard_map/ppermute | solution.py:460
  9.7 5.5 %prepare.1 = (f32[256,1024]{1,0:T(8,128)}, f32[256,1024]{1,0:T(8,128)}, bf16[1024,384]{1,0:T(8,128)(2,1)}) custom-call(s32[1]{0:T(128)} %bitcast.12.refs_0_, bf16[256,1024]{1,0:T(8,128)(2,1)} %bitcast.37, bf16[256,1024]{1,0:T(8,128)(2,1)} %norm.1.refs_2_.refs_1_.refs_3_, bf16[1024,1024]{1,0:T(8,128)(2,1)} %refs_6_.1, bf16[1024,4096]{1,0:T(8,128)(2,1)} %refs_2_.1), custom_call_target="tpu_custom_call" | custom-call | flops 1073741824 | bytes 14417924 | tf_op jit(solution)/shard_map/prepare/pallas_call | solution.py:128
  18.1 1.7 %collective-permute-done.refs_2_.refs_4_ = bf16[256,1024]{1,0:T(8,128)(2,1)S(1)} collective-permute-done((bf16[256,1024]{1,0:T(8,128)(2,1)}, bf16[256,1024]{1,0:T(8,128)(2,1)S(1)}, u32[]{:S(2)}, u32[]{:S(2)}) %collective-permute-start) | collective-permute-done | bytes 524320 | tf_op jit(solution)/shard_map/ppermute | solution.py:460
  19.7 1.7 %collective-permute-start.3 = (bf16[256,1024]{1,0:T(8,128)(2,1)S(1)}, bf16[256,1024]{1,0:T(8,128)(2,1)S(1)}, u32[]{:S(2)}, u32[]{:S(2)}) collective-permute-start(bf16[256,1024]{1,0:T(8,128)(2,1)S(1)} %collective-permute-done.2.refs_4_.refs_6_), channel_id=1, source_target_pairs={{0,1},{1,0},{2,3},{3,2},{4,5},{5,4},{6,7},{7,6},{8,9},{9,8},{10,11... | collective-permute-start | bytes 1572872 | tf_op jit(solution)/shard_map/ppermute | solution.py:460
  21.5 1.6 %collective-permute-start.4 = (bf16[128,1024]{1,0:T(8,128)(2,1)S(1)}, bf16[128,1024]{1,0:T(8,128)(2,1)S(1)}, u32[]{:S(2)}, u32[]{:S(2)}) collective-permute-start(bf16[128,1024]{1,0:T(8,128)(2,1)S(1)} %slice.19), channel_id=1, source_target_pairs={{0,6},{1,7},{2,0},{3,1},{4,2},{5,3},{6,4},{7,5},{8,14},{9,15},{10,... | collective-permute-start | bytes 786440 | tf_op jit(solution)/shard_map/ppermute | solution.py:456
  25.2 4.6 %early.1 = (bf16[1024,384]{1,0:T(8,128)(2,1)}, bf16[1024,384]{1,0:T(8,128)(2,1)}) custom-call(bf16[1024,384]{1,0:T(8,128)(2,1)} %get-tuple-element.37.refs_0_.refs_1_, bf16[256,1024]{1,0:T(8,128)(2,1)} %norm.1.refs_2_.refs_1_.refs_3_, bf16[256,1024]{1,0:T(8,128)(2,1)} %copy-done.5, bf16[256,1024]{1,0:T(8,128)(2,1)} %copy-done.4, bf16[256,1024]{1,0:T(8,128)(2,1)} %copy-done.3), custom_call_target="tpu_custom_call" | custom-call | tf_op jit(solution)/shard_map/early/pallas_call | solution.py:128
  31.1 3.2 %collective-permute-done.3.refs_8_.refs_9_ = bf16[256,1024]{1,0:T(8,128)(2,1)S(1)} collective-permute-done((bf16[256,1024]{1,0:T(8,128)(2,1)S(1)}, bf16[256,1024]{1,0:T(8,128)(2,1)S(1)}, u32[]{:S(2)}, u32[]{:S(2)}) %collective-permute-start.3) | collective-permute-done | bytes 524320 | tf_op jit(solution)/shard_map/ppermute | solution.py:460
  35.4 2.5 %collective-permute-done.7.refs_10_.refs_11_ = bf16[128,1024]{1,0:T(8,128)(2,1)S(1)} collective-permute-done((bf16[128,1024]{1,0:T(8,128)(2,1)S(1)}, bf16[128,1024]{1,0:T(8,128)(2,1)S(1)}, u32[]{:S(2)}, u32[]{:S(2)}) %collective-permute-start.7) | collective-permute-done | bytes 262176 | tf_op jit(solution)/shard_map/ppermute | solution.py:460
  39.0 3.1 %collective-permute-done.8.refs_11_.refs_12_ = bf16[128,1024]{1,0:T(8,128)(2,1)S(1)} collective-permute-done((bf16[128,1024]{1,0:T(8,128)(2,1)S(1)}, bf16[128,1024]{1,0:T(8,128)(2,1)S(1)}, u32[]{:S(2)}, u32[]{:S(2)}) %collective-permute-start.8) | collective-permute-done | bytes 262176 | tf_op jit(solution)/shard_map/ppermute | solution.py:456
  42.9 9.4 %forward.1 = (bf16[2048,384]{1,0:T(8,128)(2,1)}, bf16[2048,384]{1,0:T(8,128)(2,1)}, bf16[8,272,128]{2,1,0:T(8,128)(2,1)}) custom-call(s32[11]{0:T(128)} %stack.47.refs_0_, bf16[1024,384]{1,0:T(8,128)(2,1)} %get-tuple-element.37.refs_0_.refs_1_, f32[1,1024]{1,0:T(1,128)} %fusion.1.refs_2_.refs_0_, bf16[2048,128]{1,0:T(8,128)(2,1)} %fusion.refs_3_.refs_1_, ...), custom_call_target="tpu_custom_call" | custom-call | flops 2147483648 | bytes 8687660 | tf_op jit(solution)/shard_map/forward/pallas_call | solution.py:128
  52.3 13.2 %all_to_all.20.refs_0_ = bf16[8,272,128]{2,1,0:T(8,128)(2,1)} all-to-all(bf16[8,272,128]{2,1,0:T(8,128)(2,1)} %get-tuple-element.48), channel_id=1, replica_groups=mesh['dp'=16,'seq'=8] {'seq'}, dimensions={0} | all-to-all | bytes 1114112 | tf_op jit(solution)/shard_map/all_to_all | solution.py:509
  65.5 4.2 %mix.1 = (bf16[8,256,256]{2,1,0:T(8,128)(2,1)}, bf16[256,1024]{1,0:T(8,128)(2,1)}, bf16[256,1024]{1,0:T(8,128)(2,1)}) custom-call(bf16[8,272,128]{2,1,0:T(8,128)(2,1)} %all_to_all.20.refs_0_, f32[256,1024]{1,0:T(8,128)} %get-tuple-element.49.refs_1_, f32[256,1024]{1,0:T(8,128)} %get-tuple-element.50.refs_2_), custom_call_target="tpu_custom_call" | custom-call | bytes 4751360 | tf_op jit(solution)/shard_map/mix/pallas_call | solution.py:128
  69.8 15.4 %all_to_all.21.refs_3_.refs_1_ = bf16[8,256,256]{2,1,0:T(8,128)(2,1)} all-to-all(bf16[8,256,256]{2,1,0:T(8,128)(2,1)} %get-tuple-element.52), channel_id=1, replica_groups=mesh['dp'=16,'seq'=8] {'seq'}, dimensions={0} | all-to-all | bytes 2097152 | tf_op jit(solution)/shard_map/all_to_all | solution.py:509
  85.1 12.4 %backward.1.refs_2_ = bf16[8,256,384]{2,1,0:T(8,128)(2,1)} custom-call(f32[1,1024]{1,0:T(1,128)} %fusion.1.refs_2_.refs_0_, bf16[2048,128]{1,0:T(8,128)(2,1)} %fusion.refs_3_.refs_1_, bf16[2048,384]{1,0:T(8,128)(2,1)} %get-tuple-element.53.refs_2_, bf16[8,256,256]{2,1,0:T(8,128)(2,1)} %all_to_all.21.refs_3_.refs_1_, bf16[2048,384]{1,0:T(8,128)(2,1)} %get-tuple-element.54.refs_4_), custom_call_target="tpu_custom_call" | custom-call | flops 10737418240 | bytes 6295552 | tf_op jit(solution)/shard_map/backward/pallas_call | solution.py:128
  97.6 3.9 %all-to-all-start.2 = ((bf16[8,256,384]{2,1,0:T(8,128)(2,1)}), bf16[8,256,384]{2,1,0:T(8,128)(2,1)S(1)}, u32[]{:S(2)}, u32[]{:S(2)}) async-start(bf16[8,256,384]{2,1,0:T(8,128)(2,1)} %backward.1.refs_2_), calls=%async_computation.2 | async-start | bytes 3145728 | tf_op jit(solution)/shard_map/all_to_all | solution.py:509
  101.4 8.7 %sums.1 = (bf16[8,64,1536]{2,1,0:T(8,128)(2,1)}, bf16[8,64,512]{2,1,0:T(8,128)(2,1)}, bf16[8,64,512]{2,1,0:T(8,128)(2,1)}, bf16[8,64,512]{2,1,0:T(8,128)(2,1)}) custom-call(s32[11]{0:T(128)} %stack.47.refs_0_, bf16[8,256,256]{2,1,0:T(8,128)(2,1)} %all_to_all.21.refs_3_.refs_1_, bf16[8,256,384]{2,1,0:T(8,128)(2,1)} %backward.1.refs_2_, ...), custom_call_target="tpu_custom_call" | custom-call | flops 2684354560 | bytes 11010092 | tf_op jit(solution)/shard_map/sums/pallas_call | solution.py:128
  110.8 1.5 collective-permute-done.9.refs_1_
  115.2 1.8 %join.1 = bf16[8,64,1536]{2,1,0:T(8,128)(2,1)} custom-call(bf16[8,64,1536]{2,1,0:T(8,128)(2,1)S(1)} %copy-done.1, bf16[8,64,512]{2,1,0:T(8,128)(2,1)S(1)} %collective-permute-done.9.refs_1_, bf16[8,64,512]{2,1,0:T(8,128)(2,1)S(1)} %collective-permute-done.10.refs_2_, bf16[8,64,512]{2,1,0:T(8,128)(2,1)S(1)} %collective-permute-done.11.refs_3_), custom_call_target="tpu_custom_call" | custom-call | tf_op jit(solution)/shard_map/join/pallas_call | solution.py:128
  118.2 10.7 %all-to-all-start.3 = ((bf16[64,8,1536]{2,1,0:T(8,128)(2,1)}), bf16[64,8,1536]{2,1,0:T(8,128)(2,1)S(1)}, u32[]{:S(2)}, u32[]{:S(2)}) async-start(bf16[64,8,1536]{2,1,0:T(8,128)(2,1)} %bitcast.20), calls=%async_computation.3 | async-start | bytes 3145728 | tf_op jit(solution)/shard_map/all_to_all | solution.py:505
  128.9 10.0 %input_grad.1 = (bf16[256,1024]{1,0:T(8,128)(2,1)}, bf16[256,1024]{1,0:T(8,128)(2,1)}) custom-call(bf16[256,1024]{1,0:T(8,128)(2,1)} %get-tuple-element.51.refs_0_, bf16[8,256,384]{2,1,0:T(8,128)(2,1)} %copy-done.2, bf16[1024,4096]{1,0:T(8,128)(2,1)} %refs_2_.1, bf16[256,1024]{1,0:T(8,128)(2,1)} %bitcast.41, bf16[256,1024]{1,0:T(8,128)(2,1)} %bitcast.39, ...), custom_call_target="tpu_custom_call" | custom-call | flops 2147483648 | bytes 15204352 | tf_op jit(solution)/shard_map/input_grad/pallas_call | solution.py:128
  138.9 14.9 %all-to-all-done.3 = bf16[64,8,1536]{2,1,0:T(8,128)(2,1)S(1)} async-done(((bf16[64,8,1536]{2,1,0:T(8,128)(2,1)}), bf16[64,8,1536]{2,1,0:T(8,128)(2,1)S(1)}, u32[]{:S(2)}, u32[]{:S(2)}) %all-to-all-start.3) | async-done | bytes 1572896 | tf_op jit(solution)/shard_map/all_to_all | solution.py:505
  (51 shorter events, 17.1 us)
Async XLA Ops:
  0.6 8.2 %copy-start = (f32[8,128]{1,0:T(8,128)S(1)}, f32[8,128]{1,0:T(8,128)}, u32[]{:S(2)}) copy-start(f32[8,128]{1,0:T(8,128)} %param.10) | copy-start | bytes 12292
  2.8 15.0 %collective-permute-start.2 = (bf16[256,1024]{1,0:T(8,128)(2,1)}, bf16[256,1024]{1,0:T(8,128)(2,1)S(1)}, u32[]{:S(2)}, u32[]{:S(2)}) collective-permute-start(bf16[256,1024]{1,0:T(8,128)(2,1)} %norm.1.refs_2_.refs_1_.refs_3_), channel_id=1, source_target_pairs={{0,2},{1,3},{2,4},{3,5},{4,6},{5,7},{6,0},{7,1},{8,10},{9,11},{10,... | collective-permute-start | bytes 1572872 | tf_op jit(solution)/shard_map/ppermute | solution.py:456
  4.5 13.6 %collective-permute-start.1 = (bf16[256,1024]{1,0:T(8,128)(2,1)}, bf16[256,1024]{1,0:T(8,128)(2,1)S(1)}, u32[]{:S(2)}, u32[]{:S(2)}) collective-permute-start(bf16[256,1024]{1,0:T(8,128)(2,1)} %norm.1.refs_2_.refs_1_.refs_3_), channel_id=1, source_target_pairs={{0,6},{1,7},{2,0},{3,1},{4,2},{5,3},{6,4},{7,5},{8,14},{9,15},{10,... | collective-permute-start | bytes 1572872 | tf_op jit(solution)/shard_map/ppermute | solution.py:456
  6.1 13.6 %collective-permute-start = (bf16[256,1024]{1,0:T(8,128)(2,1)}, bf16[256,1024]{1,0:T(8,128)(2,1)S(1)}, u32[]{:S(2)}, u32[]{:S(2)}) collective-permute-start(bf16[256,1024]{1,0:T(8,128)(2,1)} %norm.1.refs_2_.refs_1_.refs_3_), channel_id=1, source_target_pairs={{0,1},{1,0},{2,3},{3,2},{4,5},{5,4},{6,7},{7,6},{8,9},{9,8},{10,11... | collective-permute-start | bytes 1572872 | tf_op jit(solution)/shard_map/ppermute | solution.py:460
  9.7 5.5 %copy-start.7 = (s32[1,2048]{1,0:T(1,128)S(1)}, s32[1,2048]{1,0:T(1,128)}, u32[]{:S(2)}) copy-start(s32[1,2048]{1,0:T(1,128)} %param.11) | copy-start | bytes 24580
  17.9 7.4 %copy-start.3 = (bf16[256,1024]{1,0:T(8,128)(2,1)}, bf16[256,1024]{1,0:T(8,128)(2,1)S(1)}, u32[]{:S(2)}) copy-start(bf16[256,1024]{1,0:T(8,128)(2,1)S(1)} %collective-permute-done.2.refs_4_.refs_6_) | copy-start | bytes 1572868
  18.1 7.2 %copy-start.4 = (bf16[256,1024]{1,0:T(8,128)(2,1)}, bf16[256,1024]{1,0:T(8,128)(2,1)S(1)}, u32[]{:S(2)}) copy-start(bf16[256,1024]{1,0:T(8,128)(2,1)S(1)} %collective-permute-done.1.refs_3_.refs_5_) | copy-start | bytes 1572868
  19.7 5.5 %copy-start.5 = (bf16[256,1024]{1,0:T(8,128)(2,1)}, bf16[256,1024]{1,0:T(8,128)(2,1)S(1)}, u32[]{:S(2)}) copy-start(bf16[256,1024]{1,0:T(8,128)(2,1)S(1)} %collective-permute-done.refs_2_.refs_4_) | copy-start | bytes 1572868
  19.7 14.6 %collective-permute-start.3 = (bf16[256,1024]{1,0:T(8,128)(2,1)S(1)}, bf16[256,1024]{1,0:T(8,128)(2,1)S(1)}, u32[]{:S(2)}, u32[]{:S(2)}) collective-permute-start(bf16[256,1024]{1,0:T(8,128)(2,1)S(1)} %collective-permute-done.2.refs_4_.refs_6_), channel_id=1, source_target_pairs={{0,1},{1,0},{2,3},{3,2},{4,5},{5,4},{6,7},{7,6},{8,9},{9,8},{10,11... | collective-permute-start | bytes 1572872 | tf_op jit(solution)/shard_map/ppermute | solution.py:460
  21.5 9.3 %collective-permute-start.4 = (bf16[128,1024]{1,0:T(8,128)(2,1)S(1)}, bf16[128,1024]{1,0:T(8,128)(2,1)S(1)}, u32[]{:S(2)}, u32[]{:S(2)}) collective-permute-start(bf16[128,1024]{1,0:T(8,128)(2,1)S(1)} %slice.19), channel_id=1, source_target_pairs={{0,6},{1,7},{2,0},{3,1},{4,2},{5,3},{6,4},{7,5},{8,14},{9,15},{10,... | collective-permute-start | bytes 786440 | tf_op jit(solution)/shard_map/ppermute | solution.py:456
  23.1 15.9 %collective-permute-start.6 = (bf16[256,1024]{1,0:T(8,128)(2,1)S(1)}, bf16[256,1024]{1,0:T(8,128)(2,1)S(1)}, u32[]{:S(2)}, u32[]{:S(2)}) collective-permute-start(bf16[256,1024]{1,0:T(8,128)(2,1)S(1)} %collective-permute-done.refs_2_.refs_4_), channel_id=1, source_target_pairs={{0,6},{1,7},{2,0},{3,1},{4,2},{5,3},{6,4},{7,5},{8,14},{9,15},{10,... | collective-permute-start | bytes 1572872 | tf_op jit(solution)/shard_map/ppermute | solution.py:456
  23.9 11.4 %collective-permute-start.5 = (bf16[128,1024]{1,0:T(8,128)(2,1)S(1)}, bf16[128,1024]{1,0:T(8,128)(2,1)}, u32[]{:S(2)}, u32[]{:S(2)}) collective-permute-start(bf16[128,1024]{1,0:T(8,128)(2,1)S(1)} %slice.20), channel_id=1, source_target_pairs={{0,2},{1,3},{2,4},{3,5},{4,6},{5,7},{6,0},{7,1},{8,10},{9,11},{10,... | collective-permute-start | bytes 786440 | tf_op jit(solution)/shard_map/ppermute | solution.py:456
  30.8 11.4 %copy-start.9 = (bf16[128,1024]{1,0:T(8,128)(2,1)}, bf16[128,1024]{1,0:T(8,128)(2,1)S(1)}, u32[]{:S(2)}) copy-start(bf16[128,1024]{1,0:T(8,128)(2,1)S(1)} %collective-permute-done.4.refs_6_.refs_7_) | copy-start | bytes 786436
  30.8 7.0 %collective-permute-start.7 = (bf16[128,1024]{1,0:T(8,128)(2,1)S(1)}, bf16[128,1024]{1,0:T(8,128)(2,1)S(1)}, u32[]{:S(2)}, u32[]{:S(2)}) collective-permute-start(bf16[128,1024]{1,0:T(8,128)(2,1)S(1)} %collective-permute-done.4.refs_6_.refs_7_), channel_id=1, source_target_pairs={{0,1},{1,0},{2,3},{3,2},{4,5},{5,4},{6,7},{7,6},{8,9},{9,8},{10,11... | collective-permute-start | bytes 786440 | tf_op jit(solution)/shard_map/ppermute | solution.py:460
  34.3 7.9 %copy-start.6 = (bf16[256,1024]{1,0:T(8,128)(2,1)}, bf16[256,1024]{1,0:T(8,128)(2,1)S(1)}, u32[]{:S(2)}) copy-start(bf16[256,1024]{1,0:T(8,128)(2,1)S(1)} %collective-permute-done.3.refs_8_.refs_9_) | copy-start | bytes 1572868
  34.3 7.8 %collective-permute-start.8 = (bf16[128,1024]{1,0:T(8,128)(2,1)S(1)}, bf16[128,1024]{1,0:T(8,128)(2,1)S(1)}, u32[]{:S(2)}, u32[]{:S(2)}) collective-permute-start(bf16[128,1024]{1,0:T(8,128)(2,1)S(1)} %slice.21), channel_id=1, source_target_pairs={{0,2},{1,3},{2,4},{3,5},{4,6},{5,7},{6,0},{7,1},{8,10},{9,11},{10,... | collective-permute-start | bytes 786440 | tf_op jit(solution)/shard_map/ppermute | solution.py:456
  37.8 4.3 %copy-start.10 = (bf16[128,1024]{1,0:T(8,128)(2,1)}, bf16[128,1024]{1,0:T(8,128)(2,1)S(1)}, u32[]{:S(2)}) copy-start(bf16[128,1024]{1,0:T(8,128)(2,1)S(1)} %collective-permute-done.7.refs_10_.refs_11_) | copy-start | bytes 786436
  39.0 3.1 %copy-start.8 = (bf16[256,1024]{1,0:T(8,128)(2,1)}, bf16[256,1024]{1,0:T(8,128)(2,1)S(1)}, u32[]{:S(2)}) copy-start(bf16[256,1024]{1,0:T(8,128)(2,1)S(1)} %collective-permute-done.6.refs_9_.refs_10_) | copy-start | bytes 1572868
  97.6 19.5 %all-to-all-start.2 = ((bf16[8,256,384]{2,1,0:T(8,128)(2,1)}), bf16[8,256,384]{2,1,0:T(8,128)(2,1)S(1)}, u32[]{:S(2)}, u32[]{:S(2)}) async-start(bf16[8,256,384]{2,1,0:T(8,128)(2,1)} %backward.1.refs_2_), calls=%async_computation.2 | async-start | bytes 3145728 | tf_op jit(solution)/shard_map/all_to_all | solution.py:509
  110.1 2.2 %collective-permute-start.9 = (bf16[8,64,512]{2,1,0:T(8,128)(2,1)}, bf16[8,64,512]{2,1,0:T(8,128)(2,1)S(1)}, u32[]{:S(2)}, u32[]{:S(2)}) collective-permute-start(bf16[8,64,512]{2,1,0:T(8,128)(2,1)} %get-tuple-element.57), channel_id=1, source_target_pairs={{0,8},{8,0},{16,24},{24,16},{32,40},{40,32},{48,56},{56,48},{64,72... | collective-permute-start | bytes 1572872 | tf_op jit(solution)/shard_map/ppermute | solution.py:460
  110.2 2.9 %collective-permute-start.10 = (bf16[8,64,512]{2,1,0:T(8,128)(2,1)}, bf16[8,64,512]{2,1,0:T(8,128)(2,1)S(1)}, u32[]{:S(2)}, u32[]{:S(2)}) collective-permute-start(bf16[8,64,512]{2,1,0:T(8,128)(2,1)} %get-tuple-element.58), channel_id=1, source_target_pairs={{0,8},{8,0},{16,24},{24,16},{32,40},{40,32},{48,56},{56,48},{64,72... | collective-permute-start | bytes 1572872 | tf_op jit(solution)/shard_map/ppermute | solution.py:460
  110.7 3.1 %collective-permute-start.11 = (bf16[8,64,512]{2,1,0:T(8,128)(2,1)}, bf16[8,64,512]{2,1,0:T(8,128)(2,1)S(1)}, u32[]{:S(2)}, u32[]{:S(2)}) collective-permute-start(bf16[8,64,512]{2,1,0:T(8,128)(2,1)} %get-tuple-element.59), channel_id=1, source_target_pairs={{0,8},{8,0},{16,24},{24,16},{32,40},{40,32},{48,56},{56,48},{64,72... | collective-permute-start | bytes 1572872 | tf_op jit(solution)/shard_map/ppermute | solution.py:460
  113.8 1.4 copy-start.1
  118.2 35.6 %all-to-all-start.3 = ((bf16[64,8,1536]{2,1,0:T(8,128)(2,1)}), bf16[64,8,1536]{2,1,0:T(8,128)(2,1)S(1)}, u32[]{:S(2)}, u32[]{:S(2)}) async-start(bf16[64,8,1536]{2,1,0:T(8,128)(2,1)} %bitcast.20), calls=%async_computation.3 | async-start | bytes 3145728 | tf_op jit(solution)/shard_map/all_to_all | solution.py:505
  (2 other events, 1.9 us)

commit v3 on v2

--- a/solution.py
+++ b/solution.py
@@ -206,30 +206,40 @@
 
 
 def early_kernel(weight, *refs):
-    pieces, (feature, slope) = refs[:EARLY], refs[EARLY:]
+    pieces, (feature, slope) = refs[:-2], refs[-2:]
     weight_ref = weight.ready()
-    for index, piece in enumerate(pieces):
-        rows = slice(index * TILE, (index + 1) * TILE)
-        made, rate = project(piece.ready()[...], weight_ref[...])
+    first = 0
+    for piece in pieces:
+        values = piece.ready()[...]
+        rows = slice(first, first + values.shape[0])
+        made, rate = project(values, weight_ref[...])
         feature.ref[rows, :] = made
         slope.ref[rows, :] = rate
+        first += values.shape[0]
 
 
 def forward_kernel(scale, start_smem, *refs):
-    weight, table, mask, feature_early, slope_early = refs[:5]
-    pieces = refs[5 : PIECES - EARLY + 5]
-    feature, slope, attended, bias_ref, key_ref, sems = refs[PIECES - EARLY + 5 :]
+    weight, table, mask = refs[:3]
+    groups = ((refs[3], refs[4], SIZES[:EARLY]), (refs[5], refs[6], SIZES[EARLY:]))
+    done = len(SIZES)
+    pieces = refs[7 : PIECES - done + 7]
+    feature, slope, attended, bias_ref, key_ref, sems = refs[PIECES - done + 7 :]
     feature_ref, slope_ref = feature.ref, slope.ref
     count, _, head = attended.ref.shape
     reach = bias_ref.shape[0] - 1
     copies = []
-    for index in range(EARLY):
-        source = pl.ds(index * TILE, TILE)
-        rows = pl.ds(pl.multiple_of(start_smem[index], HALF), TILE)
-        for far, near in ((feature_early, feature_ref), (slope_early, slope_ref)):
-            copies.append(
-                pltpu.make_async_copy(far.at[source], near.at[rows], sems.at[len(copies)])
-            )
+    index = 0
+    for feature_far, slope_far, sizes in groups:
+        first = 0
+        for size in sizes:
+            source = pl.ds(first, size)
+            rows = pl.ds(pl.multiple_of(start_smem[index], HALF), size)
+            for far, near in ((feature_far, feature_ref), (slope_far, slope_ref)):
+                copies.append(
+                    pltpu.make_async_copy(far.at[source], near.at[rows], sems.at[len(copies)])
+                )
+            first += size
+            index += 1
     for copy in copies:
         copy.start()
     row_at = lax.broadcasted_iota(jnp.int32, (16, HALF), 0)
@@ -239,7 +249,7 @@
     weight_ref = weight.ready()
     for index, piece in enumerate(pieces):
         ref = piece.ready()
-        rows = pl.ds(pl.multiple_of(start_smem[index + EARLY], HALF), ref.shape[0])
+        rows = pl.ds(pl.multiple_of(start_smem[index + done], HALF), ref.shape[0])
         made, rate = project(ref[...], weight_ref[...])
         feature_ref[rows, :] = made
         slope_ref[rows, :] = rate
@@ -493,6 +503,7 @@
 
 PIECES = 10
 EARLY = 4
+SIZES = [256, 256, 256, 256, 128, 128, 256]
 HALF = TILE // 2
 
 
@@ -549,9 +560,13 @@
         (near, gg, gate_proj, weight, table, mask)
     )
     kept = shape((EARLY * rows, 3 * head), BF16)
+    kept_next = shape((2 * rows, 3 * head), BF16)
     early = call(early_kernel, [kept, kept], "early", light=True)(weight, half, *near)
     pieces, starts, early = gather_rest(half, *near, early)
     info = lax.optimization_barrier(jnp.stack(starts + [core]))
+    later = call(early_kernel, [kept_next, kept_next], "later", light=True)(
+        weight, *pieces[EARLY : len(SIZES)]
+    )
 
     tiles = pltpu.VMEM((reach + 1, TILE, TILE), F32)
     features, slopes, attended = call(
@@ -564,12 +579,12 @@
         "forward",
         smem=1,
         out_parts={2: 8},
-        far=(4, 5),
+        far=(4, 5, 6, 7),
         scratch=[
-            tiles, pltpu.VMEM((length, 2 * head), BF16), pltpu.SemaphoreType.DMA((2 * EARLY,))
+            tiles, pltpu.VMEM((length, 2 * head), BF16), pltpu.SemaphoreType.DMA((2 * len(SIZES),))
         ],
         flops=2 * length * width * 4 * head,
-    )(info, weight, table, mask, *early, *pieces[EARLY:])
+    )(info, weight, table, mask, *early, *later, *pieces[len(SIZES) :])
     attended_own = exchange(attended)
 
     row_shape = shape((rows, width), BF16)

time: 156 us -> 155 us (level)
  waiting for transfers between devices: 32.1 us -> 28.1 us
  Pallas kernels: 58.9 us -> 61.6 us
    pallas_call x9 -> x10, Pallas kernels: 58.9 us -> 61.6 us  [run(): pl.pallas_call(kernel, out_shape=outs, in_specs=[pl.BlockSpec(memory_spac...]
    ppermute x6, waiting for transfers between devices: 10.3 us -> 7.89 us  [swap(): lax.ppermute(values, axis, [(index, index ^ bits) for index in range(size)])]
  transfers between devices with their start and end apart: 14 -> 14, of which waited for: 12 -> 10; matrix products, arithmetic and copies ran while one was open for 2% -> 2% of each run, Pallas kernels for 20% -> 22%
where the time goes in v3:
time: 155 us
  Pallas kernels  61.6 us (40%)
  blocking collectives  28.6 us (18%)
  waiting for transfers between devices  28.1 us (18%)
  starting transfers between devices  26.6 us (17%)
  local copies, waits for them, and re-layouts  6.2 us (4%)
  other arithmetic  1.97 us (1%)
    pallas_call x10, Pallas kernels, run(): pl.pallas_call(kernel, out_shape=outs, in_specs=[pl.BlockSpec(memory_spac...  61.6 us
    all_to_all x2, blocking collectives, exchange(): return lax.all_to_all(values, 'seq', 0, 0)  28.6 us
    all_to_all x1, waiting for transfers between devices, exchange_chips(): return lax.all_to_all(values, ('dp', 'seq'), 0, 0, axis_index_groups=CHIPS)  14.9 us
    all_to_all x1, starting transfers between devices, exchange_chips(): return lax.all_to_all(values, ('dp', 'seq'), 0, 0, axis_index_groups=CHIPS)  10.7 us
    ppermute x6, waiting for transfers between devices, swap(): lax.ppermute(values, axis, [(index, index ^ bits) for index in range(size)])  7.89 us
    ppermute x6, starting transfers between devices, shift(): lax.ppermute(values, 'seq', [(index, (index + by) % 8) for index in range...  7.35 us
    ppermute x6, waiting for transfers between devices, shift(): lax.ppermute(values, 'seq', [(index, (index + by) % 8) for index in range...  5.38 us
    unnamed x25, local copies, waits for them, and re-layouts  4.74 us
  transfers between devices with their start and end apart: 14, of which 10 were waited for; matrix products, arithmetic and copies ran while one was open for 2% of the time, Pallas kernels for 22%

profile of v3, /device:TPU:0, one launch (start us, length us, event | category | flops | bytes accessed | tf_op | source)
XLA Modules:
  0.0 154.9 jit_solution(15378830038350142861)
XLA Ops:
  0.6 2.2 %norm.1.refs_2_.refs_1_.refs_3_ = bf16[256,1024]{1,0:T(8,128)(2,1)} custom-call(bf16[256,1024]{1,0:T(8,128)(2,1)} %bitcast.40), custom_call_target="tpu_custom_call" | custom-call | bytes 1048576 | tf_op jit(solution)/shard_map/norm/pallas_call | solution.py:128
  2.8 1.6 %collective-permute-start.2 = (bf16[256,1024]{1,0:T(8,128)(2,1)}, bf16[256,1024]{1,0:T(8,128)(2,1)S(1)}, u32[]{:S(2)}, u32[]{:S(2)}) collective-permute-start(bf16[256,1024]{1,0:T(8,128)(2,1)} %norm.1.refs_2_.refs_1_.refs_3_), channel_id=1, source_target_pairs={{0,2},{1,3},{2,4},{3,5},{4,6},{5,7},{6,0},{7,1},{8,10},{9,11},{10,... | collective-permute-start | bytes 1572872 | tf_op jit(solution)/shard_map/ppermute | solution.py:466
  4.5 1.7 %collective-permute-start.1 = (bf16[256,1024]{1,0:T(8,128)(2,1)}, bf16[256,1024]{1,0:T(8,128)(2,1)S(1)}, u32[]{:S(2)}, u32[]{:S(2)}) collective-permute-start(bf16[256,1024]{1,0:T(8,128)(2,1)} %norm.1.refs_2_.refs_1_.refs_3_), channel_id=1, source_target_pairs={{0,6},{1,7},{2,0},{3,1},{4,2},{5,3},{6,4},{7,5},{8,14},{9,15},{10,... | collective-permute-start | bytes 1572872 | tf_op jit(solution)/shard_map/ppermute | solution.py:466
  6.1 2.0 %collective-permute-start = (bf16[256,1024]{1,0:T(8,128)(2,1)}, bf16[256,1024]{1,0:T(8,128)(2,1)S(1)}, u32[]{:S(2)}, u32[]{:S(2)}) collective-permute-start(bf16[256,1024]{1,0:T(8,128)(2,1)} %norm.1.refs_2_.refs_1_.refs_3_), channel_id=1, source_target_pairs={{0,1},{1,0},{2,3},{3,2},{4,5},{5,4},{6,7},{7,6},{8,9},{9,8},{10,11... | collective-permute-start | bytes 1572872 | tf_op jit(solution)/shard_map/ppermute | solution.py:470
  9.7 5.5 %prepare.1 = (f32[256,1024]{1,0:T(8,128)}, f32[256,1024]{1,0:T(8,128)}, bf16[1024,384]{1,0:T(8,128)(2,1)}) custom-call(s32[1]{0:T(128)} %bitcast.12.refs_0_, bf16[256,1024]{1,0:T(8,128)(2,1)} %bitcast.37, bf16[256,1024]{1,0:T(8,128)(2,1)} %norm.1.refs_2_.refs_1_.refs_3_, bf16[1024,1024]{1,0:T(8,128)(2,1)} %refs_6_.1, bf16[1024,4096]{1,0:T(8,128)(2,1)} %refs_2_.1), custom_call_target="tpu_custom_call" | custom-call | flops 1073741824 | bytes 14417924 | tf_op jit(solution)/shard_map/prepare/pallas_call | solution.py:128
  18.1 1.7 %collective-permute-done.refs_2_.refs_4_ = bf16[256,1024]{1,0:T(8,128)(2,1)S(1)} collective-permute-done((bf16[256,1024]{1,0:T(8,128)(2,1)}, bf16[256,1024]{1,0:T(8,128)(2,1)S(1)}, u32[]{:S(2)}, u32[]{:S(2)}) %collective-permute-start) | collective-permute-done | bytes 524320 | tf_op jit(solution)/shard_map/ppermute | solution.py:470
  19.7 1.7 %collective-permute-start.3 = (bf16[256,1024]{1,0:T(8,128)(2,1)S(1)}, bf16[256,1024]{1,0:T(8,128)(2,1)S(1)}, u32[]{:S(2)}, u32[]{:S(2)}) collective-permute-start(bf16[256,1024]{1,0:T(8,128)(2,1)S(1)} %collective-permute-done.2.refs_4_.refs_6_), channel_id=1, source_target_pairs={{0,1},{1,0},{2,3},{3,2},{4,5},{5,4},{6,7},{7,6},{8,9},{9,8},{10,11... | collective-permute-start | bytes 1572872 | tf_op jit(solution)/shard_map/ppermute | solution.py:470
  21.5 1.6 %collective-permute-start.4 = (bf16[128,1024]{1,0:T(8,128)(2,1)S(1)}, bf16[128,1024]{1,0:T(8,128)(2,1)S(1)}, u32[]{:S(2)}, u32[]{:S(2)}) collective-permute-start(bf16[128,1024]{1,0:T(8,128)(2,1)S(1)} %slice.19), channel_id=1, source_target_pairs={{0,6},{1,7},{2,0},{3,1},{4,2},{5,3},{6,4},{7,5},{8,14},{9,15},{10,... | collective-permute-start | bytes 786440 | tf_op jit(solution)/shard_map/ppermute | solution.py:466
  25.2 4.6 %early.1 = (bf16[1024,384]{1,0:T(8,128)(2,1)}, bf16[1024,384]{1,0:T(8,128)(2,1)}) custom-call(bf16[1024,384]{1,0:T(8,128)(2,1)} %get-tuple-element.39.refs_0_.refs_1_, bf16[256,1024]{1,0:T(8,128)(2,1)} %norm.1.refs_2_.refs_1_.refs_3_, bf16[256,1024]{1,0:T(8,128)(2,1)} %copy-done.6, bf16[256,1024]{1,0:T(8,128)(2,1)} %copy-done.5, bf16[256,1024]{1,0:T(8,128)(2,1)} %copy-done.4), custom_call_target="tpu_custom_call" | custom-call | tf_op jit(solution)/shard_map/early/pallas_call | solution.py:128
  31.1 3.2 %collective-permute-done.3.refs_3_.refs_9_ = bf16[256,1024]{1,0:T(8,128)(2,1)S(1)} collective-permute-done((bf16[256,1024]{1,0:T(8,128)(2,1)S(1)}, bf16[256,1024]{1,0:T(8,128)(2,1)S(1)}, u32[]{:S(2)}, u32[]{:S(2)}) %collective-permute-start.3) | collective-permute-done | bytes 524320 | tf_op jit(solution)/shard_map/ppermute | solution.py:470
  36.1 3.3 %later.1 = (bf16[512,384]{1,0:T(8,128)(2,1)}, bf16[512,384]{1,0:T(8,128)(2,1)}) custom-call(bf16[1024,384]{1,0:T(8,128)(2,1)} %get-tuple-element.39.refs_0_.refs_1_, bf16[128,1024]{1,0:T(8,128)(2,1)} %copy-done.7, bf16[128,1024]{1,0:T(8,128)(2,1)} %copy-done.8, bf16[256,1024]{1,0:T(8,128)(2,1)} %copy-done.3), custom_call_target="tpu_custom_call" | custom-call | tf_op jit(solution)/shard_map/later/pallas_call | solution.py:128
  39.4 2.7 %collective-permute-done.8.refs_10_.refs_12_ = bf16[128,1024]{1,0:T(8,128)(2,1)S(1)} collective-permute-done((bf16[128,1024]{1,0:T(8,128)(2,1)S(1)}, bf16[128,1024]{1,0:T(8,128)(2,1)S(1)}, u32[]{:S(2)}, u32[]{:S(2)}) %collective-permute-start.8) | collective-permute-done | bytes 262176 | tf_op jit(solution)/shard_map/ppermute | solution.py:466
  42.9 8.8 %forward.1 = (bf16[2048,384]{1,0:T(8,128)(2,1)}, bf16[2048,384]{1,0:T(8,128)(2,1)}, bf16[8,272,128]{2,1,0:T(8,128)(2,1)}) custom-call(s32[11]{0:T(128)} %stack.47.refs_0_, bf16[1024,384]{1,0:T(8,128)(2,1)} %get-tuple-element.39.refs_0_.refs_1_, f32[1,1024]{1,0:T(1,128)} %fusion.1.refs_2_.refs_0_, bf16[2048,128]{1,0:T(8,128)(2,1)} %fusion.refs_3_.refs_1_, ...), custom_call_target="tpu_custom_call" | custom-call | flops 2147483648 | bytes 8425516 | tf_op jit(solution)/shard_map/forward/pallas_call | solution.py:128
  51.7 13.2 %all_to_all.20.refs_0_ = bf16[8,272,128]{2,1,0:T(8,128)(2,1)} all-to-all(bf16[8,272,128]{2,1,0:T(8,128)(2,1)} %get-tuple-element.52), channel_id=1, replica_groups=mesh['dp'=16,'seq'=8] {'seq'}, dimensions={0} | all-to-all | bytes 1114112 | tf_op jit(solution)/shard_map/all_to_all | solution.py:520
  64.9 4.2 %mix.1 = (bf16[8,256,256]{2,1,0:T(8,128)(2,1)}, bf16[256,1024]{1,0:T(8,128)(2,1)}, bf16[256,1024]{1,0:T(8,128)(2,1)}) custom-call(bf16[8,272,128]{2,1,0:T(8,128)(2,1)} %all_to_all.20.refs_0_, f32[256,1024]{1,0:T(8,128)} %get-tuple-element.53.refs_1_, f32[256,1024]{1,0:T(8,128)} %get-tuple-element.54.refs_2_), custom_call_target="tpu_custom_call" | custom-call | bytes 4751360 | tf_op jit(solution)/shard_map/mix/pallas_call | solution.py:128
  69.1 15.4 %all_to_all.21.refs_3_.refs_1_ = bf16[8,256,256]{2,1,0:T(8,128)(2,1)} all-to-all(bf16[8,256,256]{2,1,0:T(8,128)(2,1)} %get-tuple-element.56), channel_id=1, replica_groups=mesh['dp'=16,'seq'=8] {'seq'}, dimensions={0} | all-to-all | bytes 2097152 | tf_op jit(solution)/shard_map/all_to_all | solution.py:520
  84.5 12.4 %backward.1.refs_2_ = bf16[8,256,384]{2,1,0:T(8,128)(2,1)} custom-call(f32[1,1024]{1,0:T(1,128)} %fusion.1.refs_2_.refs_0_, bf16[2048,128]{1,0:T(8,128)(2,1)} %fusion.refs_3_.refs_1_, bf16[2048,384]{1,0:T(8,128)(2,1)} %get-tuple-element.57.refs_2_, bf16[8,256,256]{2,1,0:T(8,128)(2,1)} %all_to_all.21.refs_3_.refs_1_, bf16[2048,384]{1,0:T(8,128)(2,1)} %get-tuple-element.58.refs_4_), custom_call_target="tpu_custom_call" | custom-call | flops 10737418240 | bytes 6295552 | tf_op jit(solution)/shard_map/backward/pallas_call | solution.py:128
  97.0 3.9 %all-to-all-start.2 = ((bf16[8,256,384]{2,1,0:T(8,128)(2,1)}), bf16[8,256,384]{2,1,0:T(8,128)(2,1)S(1)}, u32[]{:S(2)}, u32[]{:S(2)}) async-start(bf16[8,256,384]{2,1,0:T(8,128)(2,1)} %backward.1.refs_2_), calls=%async_computation.2 | async-start | bytes 3145728 | tf_op jit(solution)/shard_map/all_to_all | solution.py:520
  100.8 8.7 %sums.1 = (bf16[8,64,1536]{2,1,0:T(8,128)(2,1)}, bf16[8,64,512]{2,1,0:T(8,128)(2,1)}, bf16[8,64,512]{2,1,0:T(8,128)(2,1)}, bf16[8,64,512]{2,1,0:T(8,128)(2,1)}) custom-call(s32[11]{0:T(128)} %stack.47.refs_0_, bf16[8,256,256]{2,1,0:T(8,128)(2,1)} %all_to_all.21.refs_3_.refs_1_, bf16[8,256,384]{2,1,0:T(8,128)(2,1)} %backward.1.refs_2_, ...), custom_call_target="tpu_custom_call" | custom-call | flops 2684354560 | bytes 11010092 | tf_op jit(solution)/shard_map/sums/pallas_call | solution.py:128
  110.2 1.5 collective-permute-done.9.refs_1_
  114.6 1.8 %join.1 = bf16[8,64,1536]{2,1,0:T(8,128)(2,1)} custom-call(bf16[8,64,1536]{2,1,0:T(8,128)(2,1)S(1)} %copy-done.1, bf16[8,64,512]{2,1,0:T(8,128)(2,1)S(1)} %collective-permute-done.9.refs_1_, bf16[8,64,512]{2,1,0:T(8,128)(2,1)S(1)} %collective-permute-done.10.refs_2_, bf16[8,64,512]{2,1,0:T(8,128)(2,1)S(1)} %collective-permute-done.11.refs_3_), custom_call_target="tpu_custom_call" | custom-call | tf_op jit(solution)/shard_map/join/pallas_call | solution.py:128
  117.6 10.7 %all-to-all-start.3 = ((bf16[64,8,1536]{2,1,0:T(8,128)(2,1)}), bf16[64,8,1536]{2,1,0:T(8,128)(2,1)S(1)}, u32[]{:S(2)}, u32[]{:S(2)}) async-start(bf16[64,8,1536]{2,1,0:T(8,128)(2,1)} %bitcast.20), calls=%async_computation.3 | async-start | bytes 3145728 | tf_op jit(solution)/shard_map/all_to_all | solution.py:516
  128.3 10.0 %input_grad.1 = (bf16[256,1024]{1,0:T(8,128)(2,1)}, bf16[256,1024]{1,0:T(8,128)(2,1)}) custom-call(bf16[256,1024]{1,0:T(8,128)(2,1)} %get-tuple-element.55.refs_0_, bf16[8,256,384]{2,1,0:T(8,128)(2,1)} %copy-done.2, bf16[1024,4096]{1,0:T(8,128)(2,1)} %refs_2_.1, bf16[256,1024]{1,0:T(8,128)(2,1)} %bitcast.41, bf16[256,1024]{1,0:T(8,128)(2,1)} %bitcast.39, ...), custom_call_target="tpu_custom_call" | custom-call | flops 2147483648 | bytes 15204352 | tf_op jit(solution)/shard_map/input_grad/pallas_call | solution.py:128
  138.3 14.9 %all-to-all-done.3 = bf16[64,8,1536]{2,1,0:T(8,128)(2,1)S(1)} async-done(((bf16[64,8,1536]{2,1,0:T(8,128)(2,1)}), bf16[64,8,1536]{2,1,0:T(8,128)(2,1)S(1)}, u32[]{:S(2)}, u32[]{:S(2)}) %all-to-all-start.3) | async-done | bytes 1572896 | tf_op jit(solution)/shard_map/all_to_all | solution.py:516
  (52 shorter events, 16.6 us)
Async XLA Ops:
  0.6 8.2 %copy-start = (f32[8,128]{1,0:T(8,128)S(1)}, f32[8,128]{1,0:T(8,128)}, u32[]{:S(2)}) copy-start(f32[8,128]{1,0:T(8,128)} %param.10) | copy-start | bytes 12292
  2.8 15.0 %collective-permute-start.2 = (bf16[256,1024]{1,0:T(8,128)(2,1)}, bf16[256,1024]{1,0:T(8,128)(2,1)S(1)}, u32[]{:S(2)}, u32[]{:S(2)}) collective-permute-start(bf16[256,1024]{1,0:T(8,128)(2,1)} %norm.1.refs_2_.refs_1_.refs_3_), channel_id=1, source_target_pairs={{0,2},{1,3},{2,4},{3,5},{4,6},{5,7},{6,0},{7,1},{8,10},{9,11},{10,... | collective-permute-start | bytes 1572872 | tf_op jit(solution)/shard_map/ppermute | solution.py:466
  4.5 13.6 %collective-permute-start.1 = (bf16[256,1024]{1,0:T(8,128)(2,1)}, bf16[256,1024]{1,0:T(8,128)(2,1)S(1)}, u32[]{:S(2)}, u32[]{:S(2)}) collective-permute-start(bf16[256,1024]{1,0:T(8,128)(2,1)} %norm.1.refs_2_.refs_1_.refs_3_), channel_id=1, source_target_pairs={{0,6},{1,7},{2,0},{3,1},{4,2},{5,3},{6,4},{7,5},{8,14},{9,15},{10,... | collective-permute-start | bytes 1572872 | tf_op jit(solution)/shard_map/ppermute | solution.py:466
  6.1 13.6 %collective-permute-start = (bf16[256,1024]{1,0:T(8,128)(2,1)}, bf16[256,1024]{1,0:T(8,128)(2,1)S(1)}, u32[]{:S(2)}, u32[]{:S(2)}) collective-permute-start(bf16[256,1024]{1,0:T(8,128)(2,1)} %norm.1.refs_2_.refs_1_.refs_3_), channel_id=1, source_target_pairs={{0,1},{1,0},{2,3},{3,2},{4,5},{5,4},{6,7},{7,6},{8,9},{9,8},{10,11... | collective-permute-start | bytes 1572872 | tf_op jit(solution)/shard_map/ppermute | solution.py:470
  9.7 5.5 %copy-start.9 = (s32[1,2048]{1,0:T(1,128)S(1)}, s32[1,2048]{1,0:T(1,128)}, u32[]{:S(2)}) copy-start(s32[1,2048]{1,0:T(1,128)} %param.11) | copy-start | bytes 24580
  17.9 7.4 %copy-start.4 = (bf16[256,1024]{1,0:T(8,128)(2,1)}, bf16[256,1024]{1,0:T(8,128)(2,1)S(1)}, u32[]{:S(2)}) copy-start(bf16[256,1024]{1,0:T(8,128)(2,1)S(1)} %collective-permute-done.2.refs_4_.refs_6_) | copy-start | bytes 1572868
  18.1 7.2 %copy-start.5 = (bf16[256,1024]{1,0:T(8,128)(2,1)}, bf16[256,1024]{1,0:T(8,128)(2,1)S(1)}, u32[]{:S(2)}) copy-start(bf16[256,1024]{1,0:T(8,128)(2,1)S(1)} %collective-permute-done.1.refs_3_.refs_5_) | copy-start | bytes 1572868
  19.7 5.5 %copy-start.6 = (bf16[256,1024]{1,0:T(8,128)(2,1)}, bf16[256,1024]{1,0:T(8,128)(2,1)S(1)}, u32[]{:S(2)}) copy-start(bf16[256,1024]{1,0:T(8,128)(2,1)S(1)} %collective-permute-done.refs_2_.refs_4_) | copy-start | bytes 1572868
  19.7 14.6 %collective-permute-start.3 = (bf16[256,1024]{1,0:T(8,128)(2,1)S(1)}, bf16[256,1024]{1,0:T(8,128)(2,1)S(1)}, u32[]{:S(2)}, u32[]{:S(2)}) collective-permute-start(bf16[256,1024]{1,0:T(8,128)(2,1)S(1)} %collective-permute-done.2.refs_4_.refs_6_), channel_id=1, source_target_pairs={{0,1},{1,0},{2,3},{3,2},{4,5},{5,4},{6,7},{7,6},{8,9},{9,8},{10,11... | collective-permute-start | bytes 1572872 | tf_op jit(solution)/shard_map/ppermute | solution.py:470
  21.5 9.3 %collective-permute-start.4 = (bf16[128,1024]{1,0:T(8,128)(2,1)S(1)}, bf16[128,1024]{1,0:T(8,128)(2,1)S(1)}, u32[]{:S(2)}, u32[]{:S(2)}) collective-permute-start(bf16[128,1024]{1,0:T(8,128)(2,1)S(1)} %slice.19), channel_id=1, source_target_pairs={{0,6},{1,7},{2,0},{3,1},{4,2},{5,3},{6,4},{7,5},{8,14},{9,15},{10,... | collective-permute-start | bytes 786440 | tf_op jit(solution)/shard_map/ppermute | solution.py:466
  23.1 16.3 %collective-permute-start.6 = (bf16[256,1024]{1,0:T(8,128)(2,1)S(1)}, bf16[256,1024]{1,0:T(8,128)(2,1)}, u32[]{:S(2)}, u32[]{:S(2)}) collective-permute-start(bf16[256,1024]{1,0:T(8,128)(2,1)S(1)} %collective-permute-done.refs_2_.refs_4_), channel_id=1, source_target_pairs={{0,6},{1,7},{2,0},{3,1},{4,2},{5,3},{6,4},{7,5},{8,14},{9,15},{10,... | collective-permute-start | bytes 1572872 | tf_op jit(solution)/shard_map/ppermute | solution.py:466
  23.9 11.4 %collective-permute-start.5 = (bf16[128,1024]{1,0:T(8,128)(2,1)S(1)}, bf16[128,1024]{1,0:T(8,128)(2,1)S(1)}, u32[]{:S(2)}, u32[]{:S(2)}) collective-permute-start(bf16[128,1024]{1,0:T(8,128)(2,1)S(1)} %slice.20), channel_id=1, source_target_pairs={{0,2},{1,3},{2,4},{3,5},{4,6},{5,7},{6,0},{7,1},{8,10},{9,11},{10,... | collective-permute-start | bytes 786440 | tf_op jit(solution)/shard_map/ppermute | solution.py:466
  30.8 4.6 %copy-start.7 = (bf16[128,1024]{1,0:T(8,128)(2,1)}, bf16[128,1024]{1,0:T(8,128)(2,1)S(1)}, u32[]{:S(2)}) copy-start(bf16[128,1024]{1,0:T(8,128)(2,1)S(1)} %collective-permute-done.4.refs_1_.refs_7_) | copy-start | bytes 786436
  30.8 8.6 %collective-permute-start.7 = (bf16[128,1024]{1,0:T(8,128)(2,1)S(1)}, bf16[128,1024]{1,0:T(8,128)(2,1)S(1)}, u32[]{:S(2)}, u32[]{:S(2)}) collective-permute-start(bf16[128,1024]{1,0:T(8,128)(2,1)S(1)} %collective-permute-done.4.refs_1_.refs_7_), channel_id=1, source_target_pairs={{0,1},{1,0},{2,3},{3,2},{4,5},{5,4},{6,7},{7,6},{8,9},{9,8},{10,11... | collective-permute-start | bytes 786440 | tf_op jit(solution)/shard_map/ppermute | solution.py:470
  34.3 1.0 copy-start.3
  34.3 7.8 %collective-permute-start.8 = (bf16[128,1024]{1,0:T(8,128)(2,1)S(1)}, bf16[128,1024]{1,0:T(8,128)(2,1)S(1)}, u32[]{:S(2)}, u32[]{:S(2)}) collective-permute-start(bf16[128,1024]{1,0:T(8,128)(2,1)S(1)} %slice.21), channel_id=1, source_target_pairs={{0,2},{1,3},{2,4},{3,5},{4,6},{5,7},{6,0},{7,1},{8,10},{9,11},{10,... | collective-permute-start | bytes 786440 | tf_op jit(solution)/shard_map/ppermute | solution.py:466
  39.4 2.8 %copy-start.10 = (bf16[128,1024]{1,0:T(8,128)(2,1)}, bf16[128,1024]{1,0:T(8,128)(2,1)S(1)}, u32[]{:S(2)}) copy-start(bf16[128,1024]{1,0:T(8,128)(2,1)S(1)} %collective-permute-done.7.refs_9_.refs_11_) | copy-start | bytes 786436
  97.0 19.5 %all-to-all-start.2 = ((bf16[8,256,384]{2,1,0:T(8,128)(2,1)}), bf16[8,256,384]{2,1,0:T(8,128)(2,1)S(1)}, u32[]{:S(2)}, u32[]{:S(2)}) async-start(bf16[8,256,384]{2,1,0:T(8,128)(2,1)} %backward.1.refs_2_), calls=%async_computation.2 | async-start | bytes 3145728 | tf_op jit(solution)/shard_map/all_to_all | solution.py:520
  109.5 2.2 %collective-permute-start.9 = (bf16[8,64,512]{2,1,0:T(8,128)(2,1)}, bf16[8,64,512]{2,1,0:T(8,128)(2,1)S(1)}, u32[]{:S(2)}, u32[]{:S(2)}) collective-permute-start(bf16[8,64,512]{2,1,0:T(8,128)(2,1)} %get-tuple-element.61), channel_id=1, source_target_pairs={{0,8},{8,0},{16,24},{24,16},{32,40},{40,32},{48,56},{56,48},{64,72... | collective-permute-start | bytes 1572872 | tf_op jit(solution)/shard_map/ppermute | solution.py:470
  109.6 2.9 %collective-permute-start.10 = (bf16[8,64,512]{2,1,0:T(8,128)(2,1)}, bf16[8,64,512]{2,1,0:T(8,128)(2,1)S(1)}, u32[]{:S(2)}, u32[]{:S(2)}) collective-permute-start(bf16[8,64,512]{2,1,0:T(8,128)(2,1)} %get-tuple-element.62), channel_id=1, source_target_pairs={{0,8},{8,0},{16,24},{24,16},{32,40},{40,32},{48,56},{56,48},{64,72... | collective-permute-start | bytes 1572872 | tf_op jit(solution)/shard_map/ppermute | solution.py:470
  110.1 3.1 %collective-permute-start.11 = (bf16[8,64,512]{2,1,0:T(8,128)(2,1)}, bf16[8,64,512]{2,1,0:T(8,128)(2,1)S(1)}, u32[]{:S(2)}, u32[]{:S(2)}) collective-permute-start(bf16[8,64,512]{2,1,0:T(8,128)(2,1)} %get-tuple-element.63), channel_id=1, source_target_pairs={{0,8},{8,0},{16,24},{24,16},{32,40},{40,32},{48,56},{56,48},{64,72... | collective-permute-start | bytes 1572872 | tf_op jit(solution)/shard_map/ppermute | solution.py:470
  113.2 1.4 copy-start.1
  116.5 1.1 copy-start.2
  117.6 35.6 %all-to-all-start.3 = ((bf16[64,8,1536]{2,1,0:T(8,128)(2,1)}), bf16[64,8,1536]{2,1,0:T(8,128)(2,1)S(1)}, u32[]{:S(2)}, u32[]{:S(2)}) async-start(bf16[64,8,1536]{2,1,0:T(8,128)(2,1)} %bitcast.20), calls=%async_computation.3 | async-start | bytes 3145728 | tf_op jit(solution)/shard_map/all_to_all | solution.py:516
  (2 other events, 1.4 us)
